TPU v7x, 512 devices: a whole 4x4x16 slice. The times are simulated.
512 devices in a mesh: fsdp: 64 (over x_lo, z, core), tensor: 8 (over y, x_hi).
Axes of the slice: x: 4 (x_hi: 2, x_lo: 2; x = x_hi * 2 + x_lo), y: 4, z: 16, core: 2. Of those that a mesh axis runs over, the one named last changes fastest.
Arguments:
- tokens: bfloat16 [1344, 8192], P(None, 'tensor'), may hold values from -6 to 6
- gate_level_index: int32 [16384, 8192], P(('fsdp', 'tensor')), may hold values from 0 to 15
- upward_level_index: int32 [16384, 8192], P(('fsdp', 'tensor')), may hold values from 0 to 15
- gate_block_powers: int32 [16384, 128], P(('fsdp', 'tensor')), may hold values from -8 to -4
- upward_block_powers: int32 [16384, 128], P(('fsdp', 'tensor')), may hold values from -8 to -4
- gate_adapter_upward: bfloat16 [16384, 128], P(('fsdp', 'tensor')), may hold values from -0.5 to 0.5
- upward_adapter_upward: bfloat16 [16384, 128], P(('fsdp', 'tensor')), may hold values from -0.5 to 0.5
- gate_adapter_down: bfloat16 [128, 8192], P('fsdp', 'tensor'), may hold values from -0.0625 to 0.0625
- upward_adapter_down: bfloat16 [128, 8192], P('fsdp', 'tensor'), may hold values from -0.0625 to 0.0625
Outputs:
- activated: bfloat16 [1344, 16384], P('tensor', 'fsdp')
All inputs are finite; a program needn't handle non-finite values.
Results may differ from a plain program's by a relative error of at most 0.023.
Values may be sent and summed in bfloat16 or wider, within the bound.
No kernel may reach another device: no remote copies, remote signals or barrier semaphores. Data moves between devices by JAX's collectives and lax.ppermute only.
A program may use at most 64 MiB of HBM per device.

v0:
```python
import jax
import jax.numpy as jnp
from jax import lax
from jax.sharding import PartitionSpec as P

BLOCK = 64


NF4_LEVELS = (
    -1.0,
    -0.6961928009986877,
    -0.5250730514526367,
    -0.39491748809814453,
    -0.28444138169288635,
    -0.18477343022823334,
    -0.09105003625154495,
    0.0,
    0.07958029955625534,
    0.16093020141124725,
    0.24611230194568634,
    0.3379152408981323,
    0.44070982933044434,
    0.5626170039176941,
    0.7229568362236023,
    1.0,
)
adapter_scale = 1.0


def level_table():
    table = jnp.asarray(NF4_LEVELS, jnp.float32).astype(jnp.bfloat16)
    table = lax.optimization_barrier(table)
    return table.astype(jnp.float32)


def decode_quantized(codes, exponents):
    table = level_table()
    values = jnp.zeros(codes.shape, jnp.float32)
    for level in range(16):
        values = values + jnp.where(codes == level, table[level], 0.0)
    scales = jnp.exp2(exponents.astype(jnp.float32))
    nrows, ncols = codes.shape
    blocked = values.reshape(nrows, ncols // BLOCK, BLOCK) * scales[:, :, None]
    return blocked.reshape(nrows, ncols).astype(jnp.bfloat16)


def combine_weight(base_matrix, factor_b, factor_a):
    adapter_update = jnp.dot(factor_b, factor_a, preferred_element_type=jnp.float32)
    return (base_matrix.astype(jnp.float32) + adapter_scale * adapter_update).astype(jnp.bfloat16)


def per_device(
    tokens,
    gate_level_index,
    upward_level_index,
    gate_block_powers,
    upward_block_powers,
    gate_adapter_upward,
    upward_adapter_upward,
    gate_adapter_down,
    upward_adapter_down,
):
    gate_base_matrix = decode_quantized(gate_level_index, gate_block_powers)
    upward_base_matrix = decode_quantized(upward_level_index, upward_block_powers)
    gate_cols, up_cols = (
        lax.all_gather(gate_adapter_down, "tensor", axis=1, tiled=True),
        lax.all_gather(upward_adapter_down, "tensor", axis=1, tiled=True),
    )
    gate_complete, upward_complete = (
        lax.all_gather(gate_cols, "fsdp", axis=0, tiled=True),
        lax.all_gather(up_cols, "fsdp", axis=0, tiled=True),
    )
    gate_combined = combine_weight(gate_base_matrix, gate_adapter_upward, gate_complete)
    upward_combined = combine_weight(upward_base_matrix, upward_adapter_upward, upward_complete)
    gate_group, up_group = (
        lax.all_to_all(gate_combined, "tensor", split_axis=1, concat_axis=0, tiled=True),
        lax.all_to_all(upward_combined, "tensor", split_axis=1, concat_axis=0, tiled=True),
    )
    hidden_local = gate_group.shape[0]
    weights = jnp.concatenate([gate_group, up_group], axis=0)
    summed = lax.psum_scatter(
        lax.dot_general(
            tokens, weights, (((1,), (1,)), ((), ())), preferred_element_type=jnp.float32
        ).astype(jnp.bfloat16),
        "tensor",
        scatter_dimension=0,
        tiled=True,
    ).astype(jnp.float32)
    gate_pre = summed[:, :hidden_local]
    up_pre = summed[:, hidden_local:]
    return (jax.nn.silu(gate_pre) * up_pre).astype(jnp.bfloat16)


def solution(mesh):
    placed = (
        P(None, "tensor"),
        P(("fsdp", "tensor"), None),
        P(("fsdp", "tensor"), None),
        P(("fsdp", "tensor"), None),
        P(("fsdp", "tensor"), None),
        P(("fsdp", "tensor"), None),
        P(("fsdp", "tensor"), None),
        P("fsdp", "tensor"),
        P("fsdp", "tensor"),
    )
    return jax.shard_map(
        per_device, mesh=mesh, in_specs=placed, out_specs=P("tensor", "fsdp"), check_vma=False
    )
```

profile of v0, /device:TPU:1, one launch (start us, length us, event | category | flops | bytes accessed | tf_op | source)
XLA Modules:
  0.0 419.3 jit_solution(3199998444810626946)
XLA Ops:
  6.5 0.0 copy-start
  6.5 0.0 all-gather.5.cloned.1.call-start
  6.5 31.0 %all_gather.12 = bf16[2,8192]{1,0:T(2,128)(2,1)} all-gather(bf16[2,1024]{1,0:T(2,128)(2,1)} %param.18), channel_id=1, replica_groups=mesh['fsdp'=64,'tensor'=8] {'tensor'}, dimensions={1}, use_global_device_ids=true | all-gather | bytes 36864 | tf_op jit(solution)/shard_map/all_gather | solution.py:66
  37.5 0.0 all-gather.5.cloned.1.call-update
  37.5 0.0 all-gather.7.cloned.1.call-start
  37.6 29.4 %all_gather.14 = bf16[2,8192]{1,0:T(2,128)(2,1)} all-gather(bf16[2,1024]{1,0:T(2,128)(2,1)} %param.19), channel_id=1, replica_groups=mesh['fsdp'=64,'tensor'=8] {'tensor'}, dimensions={1}, use_global_device_ids=true | all-gather | bytes 36864 | tf_op jit(solution)/shard_map/all_gather | solution.py:67
  67.0 0.0 all-gather.7.cloned.1.call-update
  67.0 0.7 multiply_exponential_fusion.1
  67.8 1.9 mul.29
  69.7 0.0 copy-start.2
  69.7 3.0 mul.30
  72.7 0.0 copy-done.2
  72.7 1.9 mul.32
  74.6 0.0 copy-start.1
  74.6 2.9 mul.33
  77.6 0.0 copy-done.1
  77.6 0.7 fusion.8
  78.3 0.0 copy-start.3
  78.3 92.3 %all-gather.5.cloned.1.call-done = bf16[64,2,8192]{2,1,0:T(2,128)(2,1)} async-done(((bf16[1,2,8192]{2,1,0:T(2,128)(2,1)}), bf16[64,2,8192]{2,1,0:T(2,128)(2,1)}) %all-gather.5.cloned.1.call-update) | async-done | bytes 2097168 | tf_op jit(solution)/shard_map/all_gather | solution.py:70
  170.5 4.1 reshape.15
  174.7 0.0 copy-done.3
  174.7 14.1 %fusion = bf16[32,8192]{1,0:T(8,128)(2,1)S(1)} fusion(bf16[32,128]{1,0:T(8,128)(2,1)S(1)} %copy-done.3, bf16[128,8192]{1,0:T(8,128)(2,1)} %reshape.15, f32[32,8192]{1,0:T(8,128)} %mul.30, s32[32,8192]{1,0:T(8,128)} %param.12, f32[]{:T(128)} %bitcast.15, f32[]{:T(128)} %bitcast.14, f32[]{:T(128)} %bitcast.13, f32[]{:T(128)} %bitcast.12, f32[]{:T(128)} %bitcast.11, ...), kind=kOutput, calls=%fused_computation.2 | convolution fusion | flops 80740352 | bytes 4726848 | tf_op jit(solution)/shard_map/dot_general | solution.py:48
  188.8 0.8 copy.21
  189.6 6.1 %all-to-all-start = ((bf16[32,8,1024]{2,0,1:T(8,128)(2,1)}), bf16[32,8,1024]{2,0,1:T(8,128)(2,1)}, u32[]{:S(2)}, u32[]{:S(2)}) async-start(bf16[32,8,1024]{2,0,1:T(8,128)(2,1)} %bitcast.38), calls=%async_computation | async-start | bytes 1048576 | tf_op jit(solution)/shard_map/all_to_all | solution.py:76
  195.8 0.0 copy-start.4
  195.8 0.0 reduce-scatter.2.cloned.1.call-start
  195.8 95.6 %all-gather.7.cloned.1.call-done = bf16[64,2,8192]{2,1,0:T(2,128)(2,1)} async-done(((bf16[1,2,8192]{2,1,0:T(2,128)(2,1)}), bf16[64,2,8192]{2,1,0:T(2,128)(2,1)}) %all-gather.7.cloned.1.call-update) | async-done | bytes 2097168 | tf_op jit(solution)/shard_map/all_gather | solution.py:71
  291.4 4.1 reshape.17
  295.5 0.0 copy-done.4
  295.5 14.1 %fusion.1 = bf16[32,8192]{1,0:T(8,128)(2,1)S(1)} fusion(bf16[32,128]{1,0:T(8,128)(2,1)S(1)} %copy-done.4, bf16[128,8192]{1,0:T(8,128)(2,1)} %reshape.17, f32[32,8192]{1,0:T(8,128)} %mul.33, s32[32,8192]{1,0:T(8,128)} %param.13, f32[]{:T(128)} %bitcast.15, f32[]{:T(128)} %bitcast.14, f32[]{:T(128)} %bitcast.13, f32[]{:T(128)} %bitcast.12, f32[]{:T(128)} %bitcast.11, ...), kind=kOutput, calls=%fused_computation.3 | convolution fusion | flops 80740352 | bytes 4726848 | tf_op jit(solution)/shard_map/dot_general | solution.py:48
  309.6 0.0 all-to-all-done
  309.7 16.8 %all_to_all.38 = bf16[32,8,1024]{2,0,1:T(8,128)(2,1)S(1)} all-to-all(bf16[32,8,1024]{2,0,1:T(8,128)(2,1)S(1)} %bitcast.39), channel_id=1, replica_groups=mesh['fsdp'=64,'tensor'=8] {'tensor'}, dimensions={1} | all-to-all | bytes 1048576 | tf_op jit(solution)/shard_map/all_to_all | solution.py:77
  326.4 0.0 copy-done
  326.4 3.8 fusion.2
  330.2 0.0 reduce-scatter.2.cloned.1.call-update
  330.2 80.8 %reduce-scatter.2.cloned.1.call-done = bf16[168,512]{1,0:T(8,128)(2,1)} async-done(((bf16[1344,512]{1,0:T(8,128)(2,1)}), bf16[168,512]{1,0:T(8,128)(2,1)}) %reduce-scatter.2.cloned.1.call-update) | async-done | bytes 172048 | tf_op jit(solution)/shard_map/reduce_scatter | solution.py:81
  411.1 0.9 convert_element_type.62
  412.0 0.7 fusion.6
  (2 shorter events, 0.0 us)
Async XLA Ops:
  6.5 319.9 %copy-start = (bf16[1344,1024]{1,0:T(8,128)(2,1)S(1)}, bf16[1344,1024]{1,0:T(8,128)(2,1)}, u32[]{:S(2)}) copy-start(bf16[1344,1024]{1,0:T(8,128)(2,1)} %param.11) | copy-start | bytes 8257540
  6.5 164.0 %all-gather.5.cloned.1.call-start = ((), (), s32[]{:S(2)}) async-start(), calls=%async_computation.4 | async-start | bytes 2129920 | tf_op jit(solution)/shard_map/all_gather | solution.py:70
  37.5 253.9 %all-gather.7.cloned.1.call-start = ((), (), s32[]{:S(2)}) async-start(), calls=%async_computation.5 | async-start | bytes 2129920 | tf_op jit(solution)/shard_map/all_gather | solution.py:71
  69.7 3.0 copy-start.2
  74.6 2.9 copy-start.1
  78.3 96.4 %copy-start.3 = (bf16[32,128]{1,0:T(8,128)(2,1)S(1)}, bf16[32,128]{1,0:T(8,128)(2,1)}, u32[]{:S(2)}) copy-start(bf16[32,128]{1,0:T(8,128)(2,1)} %param.16) | copy-start | bytes 24580
  189.6 120.0 %all-to-all-start = ((bf16[32,8,1024]{2,0,1:T(8,128)(2,1)}), bf16[32,8,1024]{2,0,1:T(8,128)(2,1)}, u32[]{:S(2)}, u32[]{:S(2)}) async-start(bf16[32,8,1024]{2,0,1:T(8,128)(2,1)} %bitcast.38), calls=%async_computation | async-start | bytes 1048576 | tf_op jit(solution)/shard_map/all_to_all | solution.py:76
  195.8 99.8 %copy-start.4 = (bf16[32,128]{1,0:T(8,128)(2,1)S(1)}, bf16[32,128]{1,0:T(8,128)(2,1)}, u32[]{:S(2)}) copy-start(bf16[32,128]{1,0:T(8,128)(2,1)} %param.17) | copy-start | bytes 24580
  195.8 215.3 %reduce-scatter.2.cloned.1.call-start = ((), (), s32[]{:S(2)}) async-start(), calls=%async_computation.3 | async-start | bytes 1548288 | tf_op jit(solution)/shard_map/reduce_scatter | solution.py:81
Sparse Core Ops, SparseCore 0:
  37.7 132.8 all-gather.4
  172.7 118.6 all-gather.6
  330.4 80.6 reduce-scatter.1
where the time goes:
time: 420 us; the launch traced here: 419 us
  waiting for transfers between devices  269 us (64%)
  blocking collectives  77.1 us (18%)
  matrix products  32 us (8%)
  local copies, waits for them, and re-layouts  19.6 us (5%)
  between operations  13.2 us (3%)
  starting transfers between devices  6.22 us (1%)
    all_gather x1, waiting for transfers between devices, per_device(): lax.all_gather(up_cols, 'fsdp', axis=0, tiled=True)  95.6 us
    all_gather x1, waiting for transfers between devices, per_device(): lax.all_gather(gate_cols, 'fsdp', axis=0, tiled=True)  92.3 us
    reduce_scatter x1, waiting for transfers between devices, per_device(): lax.psum_scatter(lax.dot_general(tokens, weights, (((1,), (1,)), ((), ())...  80.8 us
    all_gather x1, blocking collectives, per_device(): lax.all_gather(gate_adapter_down, 'tensor', axis=1, tiled=True)  31 us
    all_gather x1, blocking collectives, per_device(): lax.all_gather(upward_adapter_down, 'tensor', axis=1, tiled=True)  29.4 us
    dot_general x2, matrix products, combine_weight(): jnp.dot(factor_b, factor_a, preferred_element_type=jnp.float32)  28.2 us
    all_to_all x1, blocking collectives, per_device(): lax.all_to_all(upward_combined, 'tensor', split_axis=1, concat_axis=0, ti...  16.8 us
    mul x4, local copies, waits for them, and re-layouts, decode_quantized(): blocked = values.reshape(nrows, ncols // BLOCK, BLOCK) * scales[:, :, None]  9.78 us
  transfers between devices with their start and end apart: 4, of which 3 were waited for; matrix products, arithmetic and copies ran while one was open for 12% of the time, Pallas kernels for 0%

commit v1 on v0

v1 whole, which is shorter than its diff:
```python
import jax
import jax.numpy as jnp
import ml_dtypes
from jax import lax
from jax.experimental import pallas as pl
from jax.experimental.pallas import tpu as pltpu
from jax.sharding import Mesh
from jax.sharding import PartitionSpec as P

BLOCK = 64
RANK = 128
GROUPS = 8
ROWS = 32
WIDTH = 1024
TOKENS = 1344
LANES = 128

NF4_LEVELS = (
    -1.0,
    -0.6961928009986877,
    -0.5250730514526367,
    -0.39491748809814453,
    -0.28444138169288635,
    -0.18477343022823334,
    -0.09105003625154495,
    0.0,
    0.07958029955625534,
    0.16093020141124725,
    0.24611230194568634,
    0.3379152408981323,
    0.44070982933044434,
    0.5626170039176941,
    0.7229568362236023,
    1.0,
)
LEVELS = tuple(float(ml_dtypes.bfloat16(v)) for v in NF4_LEVELS)

FSDP = ("xl", "z", "c")
TENSOR = ("y", "xh")


def lookup(table, index):
    return jnp.take_along_axis(table, index, axis=1, mode="promise_in_bounds")


def decode_kernel(gate_ids, up_ids, gate_powers, up_powers, gate_b, up_b, out):
    group = pl.program_id(0)
    lane = lax.broadcasted_iota(jnp.int32, (ROWS, LANES), 1)
    table = jnp.zeros((ROWS, LANES), jnp.float32)
    for level, value in enumerate(LEVELS):
        table = jnp.where(lane == level, value, table)
    half = lane // BLOCK
    for p, (ids, powers, factor) in enumerate(((gate_ids, gate_powers, gate_b), (up_ids, up_powers, up_b))):
        scales = (jnp.int32(1) << (powers[...] + 8)).astype(jnp.float32) * 2.0**-8
        rows = pl.ds(p * ROWS, ROWS)
        for chunk in range(WIDTH // LANES):
            columns = pl.ds(chunk * LANES, LANES)
            level = lookup(table, ids[:, columns])
            scale = lookup(scales, half + (group * (WIDTH // BLOCK) + chunk * (LANES // BLOCK)))
            out[0, rows, columns] = (level * scale).astype(jnp.bfloat16)
        out[0, rows, pl.ds(WIDTH, RANK)] = factor[...]


def decode(gate_ids, up_ids, gate_powers, up_powers, gate_b, up_b):
    whole = pl.BlockSpec((ROWS, RANK), lambda k: (0, 0))
    ids = pl.BlockSpec((ROWS, WIDTH), lambda k: (0, k))
    return pl.pallas_call(
        decode_kernel,
        grid=(GROUPS,),
        in_specs=[ids, ids, whole, whole, whole, whole],
        out_specs=pl.BlockSpec((1, 2 * ROWS, WIDTH + RANK), lambda k: (k, 0, 0)),
        out_shape=jax.ShapeDtypeStruct((GROUPS, 2 * ROWS, WIDTH + RANK), jnp.bfloat16),
        cost_estimate=pl.CostEstimate(flops=2**21, bytes_accessed=3 * 2**20, transcendentals=0),
        name="decode",
    )(gate_ids, up_ids, gate_powers, up_powers, gate_b, up_b)


def project_kernel(weights, a, tokens, out, merged):
    @pl.when(pl.program_id(0) == 0)
    def _():
        rank = lax.broadcasted_iota(jnp.int32, (RANK, 2 * RANK), 0)
        place = lax.broadcasted_iota(jnp.int32, (RANK, 2 * RANK), 1)
        inner = place % 4
        slot = place // 4
        owner = (slot // 32) * 32 + (slot % 16) * 2 + (slot // 16) % 2
        for p in range(2):
            factor = weights[:, pl.ds(p * ROWS, ROWS), pl.ds(WIDTH, RANK)].reshape(GROUPS * ROWS, RANK)
            pick = (inner // 2 == p) & (owner * 2 + inner % 2 == rank)
            spread = jnp.dot(
                factor, pick.astype(jnp.float32).astype(jnp.bfloat16), preferred_element_type=jnp.float32
            ).astype(jnp.bfloat16)
            update = jnp.dot(spread, a[...], preferred_element_type=jnp.float32)
            base = weights[:, pl.ds(p * ROWS, ROWS), pl.ds(0, WIDTH)].reshape(GROUPS * ROWS, WIDTH)
            merged[pl.ds(p * GROUPS * ROWS, GROUPS * ROWS), :] = (base.astype(jnp.float32) + update).astype(
                jnp.bfloat16
            )

    out[...] = lax.dot_general(
        tokens[...], merged[...], (((1,), (1,)), ((), ())), preferred_element_type=jnp.float32
    ).astype(jnp.bfloat16)


def project(weights, a, tokens, steps=2):
    part = TOKENS // steps
    return pl.pallas_call(
        project_kernel,
        grid=(steps,),
        in_specs=[
            pl.BlockSpec(weights.shape, lambda i: (0, 0, 0)),
            pl.BlockSpec(a.shape, lambda i: (0, 0)),
            pl.BlockSpec((part, WIDTH), lambda i: (i, 0)),
        ],
        out_specs=pl.BlockSpec((part, 2 * GROUPS * ROWS), lambda i: (i, 0)),
        out_shape=jax.ShapeDtypeStruct((TOKENS, 2 * GROUPS * ROWS), jnp.bfloat16),
        scratch_shapes=[pltpu.VMEM((2 * GROUPS * ROWS, WIDTH), jnp.bfloat16)],
        compiler_params=pltpu.CompilerParams(vmem_limit_bytes=48 * 2**20),
        cost_estimate=pl.CostEstimate(flops=2 * TOKENS * 512 * 1024, bytes_accessed=6 * 2**20, transcendentals=0),
        name="project",
    )(weights, a, tokens)


def finish_kernel(parts, out):
    total = parts[0].astype(jnp.float32)
    for k in range(1, GROUPS):
        total = total + parts[k].astype(jnp.float32)
    half = GROUPS * ROWS
    gate, up = total[:, :half], total[:, half:]
    out[...] = (gate / (1.0 + jnp.exp(-gate)) * up).astype(jnp.bfloat16)


def finish(parts):
    rows, columns = parts.shape[1], parts.shape[2] // 2
    return pl.pallas_call(
        finish_kernel,
        out_shape=jax.ShapeDtypeStruct((rows, columns), jnp.bfloat16),
        compiler_params=pltpu.CompilerParams(vmem_limit_bytes=32 * 2**20),
        cost_estimate=pl.CostEstimate(flops=2**20, bytes_accessed=3 * 2**19, transcendentals=2**16),
        name="finish",
    )(parts)


def per_device(tokens, gate_ids, up_ids, gate_powers, up_powers, gate_b, up_b, gate_a, up_a):
    own_a = jnp.concatenate([gate_a, up_a], axis=0)
    copies = jnp.broadcast_to(own_a[None], (lax.axis_size("z"),) + own_a.shape)
    a = lax.all_to_all(copies, "z", 0, 0, tiled=True)
    blocks = decode(gate_ids, up_ids, gate_powers, up_powers, gate_b, up_b)
    weights = lax.all_to_all(blocks, TENSOR, 0, 0, tiled=True)
    a = lax.all_gather(a.reshape(-1, WIDTH), "c", axis=0, tiled=True)
    a = lax.all_gather(a, "xl", axis=0, tiled=True)
    parts = project(weights, a, tokens)
    parts = lax.all_to_all(parts.reshape(GROUPS, TOKENS // GROUPS, -1), TENSOR, 0, 0, tiled=True)
    return finish(parts)


def solution(mesh):
    split = Mesh(mesh.devices.reshape(2, 16, 2, 4, 2), ("xl", "z", "c", "y", "xh"))
    rows = P(FSDP + TENSOR, None)
    placed = (P(None, TENSOR), rows, rows, rows, rows, rows, rows, P(FSDP, TENSOR), P(FSDP, TENSOR))
    return jax.shard_map(per_device, mesh=split, in_specs=placed, out_specs=P(TENSOR, FSDP), check_vma=False)
```

time: 420 us -> 84.3 us (0.20)
  the two profiles are of different devices: /device:TPU:1 before, /device:TPU:32 now
where the time goes in v1:
time: 84.3 us; the launch traced here: 83.8 us
  blocking collectives  38.8 us (46%)
  starting transfers between devices  22.1 us (26%)
  Pallas kernels  10.4 us (12%)
  waiting for transfers between devices  9.24 us (11%)
  local copies, waits for them, and re-layouts  2.49 us (3%)
    all_to_all x1, blocking collectives, per_device(): lax.all_to_all(parts.reshape(GROUPS, TOKENS // GROUPS, -1), TENSOR, 0, 0,...  22.3 us
    all_to_all x1, starting transfers between devices, per_device(): a = lax.all_to_all(copies, 'z', 0, 0, tiled=True)  15.2 us
    all_gather x1, blocking collectives, per_device(): a = lax.all_gather(a, 'xl', axis=0, tiled=True)  14.5 us
    all_to_all x1, waiting for transfers between devices, per_device(): a = lax.all_to_all(copies, 'z', 0, 0, tiled=True)  7.28 us
    pallas_call x1, Pallas kernels, decode(): pl.pallas_call(decode_kernel, grid=(GROUPS,), in_specs=[ids, ids, whole,...  6.94 us
    all_to_all x1, starting transfers between devices, per_device(): weights = lax.all_to_all(blocks, TENSOR, 0, 0, tiled=True)  6.93 us
    pallas_call x1, Pallas kernels, project(): pl.pallas_call(project_kernel, grid=(steps,), in_specs=[pl.BlockSpec(weig...  2.58 us
    all_gather x1, blocking collectives, per_device(): a = lax.all_gather(a.reshape(-1, WIDTH), 'c', axis=0, tiled=True)  1.99 us
  transfers between devices with their start and end apart: 2, of which 2 were waited for; matrix products, arithmetic and copies ran while one was open for 0% of the time, Pallas kernels for 8%

profile of v1, /device:TPU:32, one launch (start us, length us, event | category | flops | bytes accessed | tf_op | source)
XLA Modules:
  0.0 83.8 jit_solution(12376038285261170641)
XLA Ops:
  0.0 0.7 pad_maximum_fusion
  0.7 0.7 broadcast_in_dim.2
  1.4 15.2 %all-to-all-start.1 = ((bf16[16,4,1024]{2,1,0:T(4,128)(2,1)}), bf16[16,4,1024]{2,1,0:T(4,128)(2,1)S(1)}, u32[]{:S(2)}, u32[]{:S(2)}) async-start(bf16[16,4,1024]{2,1,0:T(4,128)(2,1)} %broadcast_in_dim.2), calls=%async_computation.1 | async-start | bytes 262144 | tf_op jit(solution)/shard_map/all_to_all | solution.py:145
  16.6 6.9 %decode.1 = bf16[8,64,1152]{2,1,0:T(8,128)(2,1)} custom-call(s32[32,8192]{1,0:T(8,128)} %gate_ids.1, s32[32,8192]{1,0:T(8,128)} %up_ids.1, s32[32,128]{1,0:T(8,128)} %gate_powers.1, s32[32,128]{1,0:T(8,128)} %up_powers.1, bf16[32,128]{1,0:T(8,128)(2,1)} %gate_b.1, bf16[32,128]{1,0:T(8,128)(2,1)} %up_b.1), custom_call_target="tpu_custom_call" | custom-call | flops 2097152 | bytes 3145728 | tf_op jit(solution)/shard_map/decode/pallas_call | solution.py:67
  23.6 7.3 %all-to-all-done.1 = bf16[16,4,1024]{2,1,0:T(4,128)(2,1)S(1)} async-done(((bf16[16,4,1024]{2,1,0:T(4,128)(2,1)}), bf16[16,4,1024]{2,1,0:T(4,128)(2,1)S(1)}, u32[]{:S(2)}, u32[]{:S(2)}) %all-to-all-start.1) | async-done | bytes 131104 | tf_op jit(solution)/shard_map/all_to_all | solution.py:145
  30.8 6.9 %all-to-all-start = ((bf16[8,64,1152]{2,1,0:T(8,128)(2,1)}), bf16[8,64,1152]{2,1,0:T(8,128)(2,1)S(1)}, u32[]{:S(2)}, u32[]{:S(2)}) async-start(bf16[8,64,1152]{2,1,0:T(8,128)(2,1)} %decode.1), calls=%async_computation | async-start | bytes 2359296 | tf_op jit(solution)/shard_map/all_to_all | solution.py:147
  37.8 2.0 %all_gather.6 = bf16[128,1024]{1,0:T(8,128)(2,1)S(1)} all-gather(bf16[64,1024]{1,0:T(8,128)(2,1)S(1)} %reshape.7), channel_id=1, replica_groups=mesh['xl'=2,'z'=16,'c'=2,'y'=4,'xh'=2] {'c'}, dimensions={0}, use_global_device_ids=true | all-gather | bytes 393216 | tf_op jit(solution)/shard_map/all_gather | solution.py:148
  39.8 14.5 %all_gather.7.a = bf16[256,1024]{1,0:T(8,128)(2,1)S(1)} all-gather(bf16[128,1024]{1,0:T(8,128)(2,1)S(1)} %all_gather.6), channel_id=1, replica_groups=mesh['xl'=2,'z'=16,'c'=2,'y'=4,'xh'=2] {'xl'}, dimensions={0}, use_global_device_ids=true | all-gather | bytes 786432 | tf_op jit(solution)/shard_map/all_gather | solution.py:149
  54.3 2.0 %all-to-all-done.weights = bf16[8,64,1152]{2,1,0:T(8,128)(2,1)S(1)} async-done(((bf16[8,64,1152]{2,1,0:T(8,128)(2,1)}), bf16[8,64,1152]{2,1,0:T(8,128)(2,1)S(1)}, u32[]{:S(2)}, u32[]{:S(2)}) %all-to-all-start) | async-done | bytes 1179680 | tf_op jit(solution)/shard_map/all_to_all | solution.py:147
  56.3 0.0 copy-start
  56.3 1.8 %copy-done = bf16[1344,1024]{1,0:T(8,128)(2,1)S(1)} copy-done((bf16[1344,1024]{1,0:T(8,128)(2,1)S(1)}, bf16[1344,1024]{1,0:T(8,128)(2,1)}, u32[]{:S(2)}) %copy-start) | copy-done | bytes 2752536
  58.0 2.6 %project.1 = bf16[1344,512]{1,0:T(8,128)(2,1)S(1)} custom-call(bf16[8,64,1152]{2,1,0:T(8,128)(2,1)S(1)} %all-to-all-done.weights, bf16[256,1024]{1,0:T(8,128)(2,1)S(1)} %all_gather.7.a, bf16[1344,1024]{1,0:T(8,128)(2,1)S(1)} %copy-done), custom_call_target="tpu_custom_call" | custom-call | flops 1409286144 | bytes 6291456 | tf_op jit(solution)/shard_map/project/pallas_call | solution.py:105
  60.6 22.3 %all_to_all.15.parts = bf16[8,168,512]{2,1,0:T(8,128)(2,1)S(1)} all-to-all(bf16[8,168,512]{2,1,0:T(8,128)(2,1)S(1)} %bitcast.1), channel_id=1, replica_groups=mesh['xl'=2,'z'=16,'c'=2,'y'=4,'xh'=2] {'y','xh'}, dimensions={0} | all-to-all | bytes 2752512 | tf_op jit(solution)/shard_map/all_to_all | solution.py:151
  82.9 0.9 %finish.1 = bf16[168,256]{1,0:T(8,128)(2,1)} custom-call(bf16[8,168,512]{2,1,0:T(8,128)(2,1)S(1)} %all_to_all.15.parts), custom_call_target="tpu_custom_call" | custom-call | flops 1048576 | bytes 1572864 | tf_op jit(solution)/shard_map/finish/pallas_call | solution.py:133
  (1 shorter events, 0.0 us)
Async XLA Ops:
  1.4 29.4 %all-to-all-start.1 = ((bf16[16,4,1024]{2,1,0:T(4,128)(2,1)}), bf16[16,4,1024]{2,1,0:T(4,128)(2,1)S(1)}, u32[]{:S(2)}, u32[]{:S(2)}) async-start(bf16[16,4,1024]{2,1,0:T(4,128)(2,1)} %broadcast_in_dim.2), calls=%async_computation.1 | async-start | bytes 262144 | tf_op jit(solution)/shard_map/all_to_all | solution.py:145
  30.8 25.4 %all-to-all-start = ((bf16[8,64,1152]{2,1,0:T(8,128)(2,1)}), bf16[8,64,1152]{2,1,0:T(8,128)(2,1)S(1)}, u32[]{:S(2)}, u32[]{:S(2)}) async-start(bf16[8,64,1152]{2,1,0:T(8,128)(2,1)} %decode.1), calls=%async_computation | async-start | bytes 2359296 | tf_op jit(solution)/shard_map/all_to_all | solution.py:147
  56.3 1.8 %copy-start = (bf16[1344,1024]{1,0:T(8,128)(2,1)S(1)}, bf16[1344,1024]{1,0:T(8,128)(2,1)}, u32[]{:S(2)}) copy-start(bf16[1344,1024]{1,0:T(8,128)(2,1)} %tokens.1) | copy-start | bytes 8257540

commit v2 on v1

v2 whole, which is shorter than its diff:
```python
import jax
import jax.numpy as jnp
import ml_dtypes
from jax import lax
from jax.experimental import pallas as pl
from jax.experimental.pallas import tpu as pltpu
from jax.sharding import Mesh
from jax.sharding import PartitionSpec as P

BLOCK = 64
RANK = 128
GROUPS = 8
ROWS = 32
WIDTH = 1024
TOKENS = 1344
LANES = 128
PIECES = 2
SIDE = 144

NF4_LEVELS = (
    -1.0,
    -0.6961928009986877,
    -0.5250730514526367,
    -0.39491748809814453,
    -0.28444138169288635,
    -0.18477343022823334,
    -0.09105003625154495,
    0.0,
    0.07958029955625534,
    0.16093020141124725,
    0.24611230194568634,
    0.3379152408981323,
    0.44070982933044434,
    0.5626170039176941,
    0.7229568362236023,
    1.0,
)
LEVELS = tuple(float(ml_dtypes.bfloat16(v)) for v in NF4_LEVELS)

FSDP = ("xl", "z", "c")
TENSOR = ("y", "xh")
def pick(ids, low, high):
    if high - low == 1:
        return jnp.full(ids.shape, LEVELS[low], jnp.float32)
    middle = (low + high) // 2
    return jnp.where(ids < middle, pick(ids, low, middle), pick(ids, middle, high))


def lookup(table, index):
    return jnp.take_along_axis(table, index, axis=1, mode="promise_in_bounds")


def decode_kernel(gate_ids, up_ids, gate_powers, up_powers, gate_b, up_b, gate_a, up_a, out, ids, small, blocks, ready, near, sent):
    extra = [
        pltpu.make_async_copy(powers, small.at[p], near.at[p]) for p, powers in enumerate((gate_powers, up_powers))
    ]
    loads, stores = [], []
    for k in range(GROUPS):
        columns = pl.ds(k * WIDTH, WIDTH)
        loads.append(
            [pltpu.make_async_copy(ref.at[:, columns], ids.at[p, k], ready.at[p, k]) for p, ref in enumerate((gate_ids, up_ids))]
        )
    for copy in extra + sum(loads, []):
        copy.start()
    blocks[GROUPS, :, :] = jnp.zeros((2 * ROWS, WIDTH), jnp.bfloat16)
    blocks[GROUPS, pl.ds(0, ROWS), pl.ds(0, RANK)] = gate_b[...]
    blocks[GROUPS, pl.ds(ROWS, ROWS), pl.ds(0, RANK)] = up_b[...]
    blocks[GROUPS + 1, :, :] = jnp.zeros((2 * ROWS, WIDTH), jnp.bfloat16)
    blocks[GROUPS + 1, pl.ds(0, 2), :] = gate_a[...]
    blocks[GROUPS + 1, pl.ds(2, 2), :] = up_a[...]
    stores.append(pltpu.make_async_copy(blocks.at[pl.ds(GROUPS, 2)], out.at[pl.ds(GROUPS, 2)], sent.at[GROUPS]))
    stores[-1].start()
    for copy in extra:
        copy.wait()
    half = lax.broadcasted_iota(jnp.int32, (ROWS, LANES), 1) // BLOCK
    scales = [(jnp.int32(1) << (small[p] + 8)).astype(jnp.float32) * 2.0**-8 for p in range(2)]
    for k in range(GROUPS):
        for p in range(2):
            loads[k][p].wait()
            rows = pl.ds(p * ROWS, ROWS)
            for chunk in range(WIDTH // LANES):
                columns = pl.ds(chunk * LANES, LANES)
                level = pick(ids[p, k, :, columns], 0, len(LEVELS))
                scale = lookup(scales[p], half + (k * (WIDTH // BLOCK) + chunk * (LANES // BLOCK)))
                blocks[k, rows, columns] = (level * scale).astype(jnp.bfloat16)
        stores.append(pltpu.make_async_copy(blocks.at[k], out.at[k], sent.at[k]))
        stores[-1].start()
    for store in stores:
        store.wait()


def decode(*args):
    shape = (GROUPS + 2, 2 * ROWS, WIDTH)
    hbm, vmem = pl.BlockSpec(memory_space=pltpu.HBM), pl.BlockSpec(memory_space=pltpu.VMEM)
    return pl.pallas_call(
        decode_kernel,
        in_specs=[hbm] * 4 + [vmem] * 4,
        out_specs=hbm,
        out_shape=jax.ShapeDtypeStruct(shape, jnp.bfloat16),
        scratch_shapes=[
            pltpu.VMEM((2, GROUPS, ROWS, WIDTH), jnp.int32),
            pltpu.VMEM((2, ROWS, LANES), jnp.int32),
            pltpu.VMEM(shape, jnp.bfloat16),
            pltpu.SemaphoreType.DMA((2, GROUPS)),
            pltpu.SemaphoreType.DMA((2,)),
            pltpu.SemaphoreType.DMA((GROUPS + 1,)),
        ],
        compiler_params=pltpu.CompilerParams(vmem_limit_bytes=62 * 2**20),
        cost_estimate=pl.CostEstimate(flops=2**24, bytes_accessed=3 * 2**20, transcendentals=0),
        name="decode",
    )(*args)


def project_kernel(weights, tokens, out, merged, held, ready):
    part = TOKENS // PIECES
    loads = []
    for i in range(PIECES):
        loads.append(pltpu.make_async_copy(tokens.at[pl.ds(i * part, part)], held.at[pl.ds(i * part, part)], ready.at[i]))
        loads[-1].start()
    half = GROUPS * ROWS
    for q in range(4):
        merged[pl.ds(q * half, half), :] = weights[:, pl.ds(q * ROWS, ROWS), :].reshape(half, WIDTH)
    for i in range(PIECES):
        rows = pl.ds(i * part, part)
        loads[i].wait()
        for q in range(4):
            columns = pl.ds(q * half, half)
            out[rows, columns] = lax.dot_general(
                held[rows, :], merged[columns, :], (((1,), (1,)), ((), ())), preferred_element_type=jnp.float32
            ).astype(jnp.bfloat16)


def project(weights, tokens):
    place = pl.BlockSpec(memory_space=pltpu.VMEM)
    columns = 4 * GROUPS * ROWS
    return pl.pallas_call(
        project_kernel,
        in_specs=[place, pl.BlockSpec(memory_space=pltpu.HBM)],
        out_specs=place,
        out_shape=jax.ShapeDtypeStruct((TOKENS, columns), jnp.bfloat16),
        scratch_shapes=[
            pltpu.VMEM((columns, WIDTH), jnp.bfloat16),
            pltpu.VMEM((TOKENS, WIDTH), jnp.bfloat16),
            pltpu.SemaphoreType.DMA((PIECES,)),
        ],
        compiler_params=pltpu.CompilerParams(vmem_limit_bytes=40 * 2**20),
        cost_estimate=pl.CostEstimate(flops=2 * TOKENS * 1024 * 1024, bytes_accessed=8 * 2**20, transcendentals=0),
        name="project",
    )(weights, tokens)


def add_up_kernel(parts, mine, theirs):
    half = 2 * GROUPS * ROWS
    for to, columns in ((mine, pl.ds(0, half)), (theirs, pl.ds(half, half))):
        total = parts[0, :, columns].astype(jnp.float32)
        for k in range(1, GROUPS):
            total = total + parts[k, :, columns].astype(jnp.float32)
        to[...] = total


def add_up(parts):
    shape = jax.ShapeDtypeStruct((parts.shape[1], parts.shape[2] // 2), jnp.float32)
    return pl.pallas_call(
        add_up_kernel,
        out_shape=[shape, shape],
        compiler_params=pltpu.CompilerParams(vmem_limit_bytes=32 * 2**20),
        cost_estimate=pl.CostEstimate(flops=2**21, bytes_accessed=3 * 2**20, transcendentals=0),
        name="add_up",
    )(parts)


def shrink_kernel(first, second, tokens, out):
    a = jnp.concatenate([first[1, pl.ds(0, 4), :].astype(jnp.float32), second[1, pl.ds(0, 4), :].astype(jnp.float32)], axis=0)
    a = a.astype(jnp.bfloat16)
    count = TOKENS // GROUPS
    for k in range(GROUPS):
        out[k, pl.ds(0, 2 * ROWS), :] = first[0, :, pl.ds(0, RANK)]
        out[k, pl.ds(2 * ROWS, 2 * ROWS), :] = second[0, :, pl.ds(0, RANK)]
        product = lax.dot_general(a, tokens[k], (((1,), (1,)), ((), ())), preferred_element_type=jnp.float32)
        rest = jnp.concatenate([product[:, LANES:], jnp.zeros((8, 2 * LANES - count), jnp.float32)], axis=1)
        out[k, pl.ds(4 * ROWS, 16), :] = jnp.concatenate([product[:, :LANES], rest], axis=0).astype(jnp.bfloat16)


def shrink(first, second, tokens):
    side = pl.BlockSpec((2, 2 * ROWS, WIDTH), lambda i: (GROUPS // 2, 0, 0))
    return pl.pallas_call(
        shrink_kernel,
        grid=(1,),
        in_specs=[side, side, pl.BlockSpec((GROUPS, TOKENS // GROUPS, WIDTH), lambda i: (0, 0, 0))],
        out_specs=pl.BlockSpec((GROUPS, SIDE, LANES), lambda i: (0, 0, 0)),
        out_shape=jax.ShapeDtypeStruct((GROUPS, SIDE, LANES), jnp.bfloat16),
        compiler_params=pltpu.CompilerParams(vmem_limit_bytes=40 * 2**20),
        cost_estimate=pl.CostEstimate(flops=2**24, bytes_accessed=3 * 2**20, transcendentals=0),
        name="shrink",
    )(first, second, tokens.reshape(GROUPS, TOKENS // GROUPS, WIDTH))


def gather_kernel(side, out):
    total = side[0, pl.ds(4 * ROWS, 16), :].astype(jnp.float32)
    for k in range(1, GROUPS):
        total = total + side[k, pl.ds(4 * ROWS, 16), :].astype(jnp.float32)
    for z in range(out.shape[0]):
        out[z] = total.astype(jnp.bfloat16)


def copies_of(side, count):
    return pl.pallas_call(
        gather_kernel,
        out_shape=jax.ShapeDtypeStruct((count, 16, LANES), jnp.bfloat16),
        cost_estimate=pl.CostEstimate(flops=2**14, bytes_accessed=2**19, transcendentals=0),
        name="copies",
    )(side)


def grow_kernel(side, shrunk, mine, theirs):
    count = TOKENS // GROUPS
    rank = lax.broadcasted_iota(jnp.int32, (RANK, 2 * RANK), 0)
    place = lax.broadcasted_iota(jnp.int32, (RANK, 2 * RANK), 1)
    spreads = [
        ((place % 4 // 2 == p) & (place // 4 * 2 + place % 2 == rank)).astype(jnp.float32).astype(jnp.bfloat16) for p in range(2)
    ]
    values = shrunk[...].astype(jnp.float32)
    low = values[:, 0:8, :].reshape(2 * RANK, LANES).T.astype(jnp.bfloat16)
    high = values[:, 8:16, :].reshape(2 * RANK, LANES).T.astype(jnp.bfloat16)
    half = GROUPS * ROWS
    for q in range(4):
        factor = side[:, pl.ds(q * ROWS, ROWS), :].reshape(half, RANK)
        factor = jnp.dot(factor, spreads[q % 2], preferred_element_type=jnp.float32).astype(jnp.bfloat16)
        to = theirs if q < 2 else mine
        columns = pl.ds(q % 2 * half, half)
        to[pl.ds(0, LANES), columns] = lax.dot_general(
            low, factor, (((1,), (1,)), ((), ())), preferred_element_type=jnp.float32
        )
        to[pl.ds(LANES, count - LANES), columns] = lax.dot_general(
            high, factor, (((1,), (1,)), ((), ())), preferred_element_type=jnp.float32
        )[: count - LANES]


def grow(side, shrunk):
    shape = jax.ShapeDtypeStruct((TOKENS // GROUPS, 2 * GROUPS * ROWS), jnp.float32)
    return pl.pallas_call(
        grow_kernel,
        out_shape=[shape, shape],
        compiler_params=pltpu.CompilerParams(vmem_limit_bytes=32 * 2**20),
        cost_estimate=pl.CostEstimate(flops=2**25, bytes_accessed=2**20, transcendentals=0),
        name="grow",
    )(side, shrunk)


def finish_kernel(mine, other, out):
    half = GROUPS * ROWS
    gate = mine[:, :half] + other[:, :half]
    up = mine[:, half:] + other[:, half:]
    out[...] = (gate / (1.0 + jnp.exp(-gate)) * up).astype(jnp.bfloat16)


def finish(mine, other):
    return pl.pallas_call(
        finish_kernel,
        out_shape=jax.ShapeDtypeStruct((TOKENS // GROUPS, GROUPS * ROWS), jnp.bfloat16),
        compiler_params=pltpu.CompilerParams(vmem_limit_bytes=32 * 2**20),
        cost_estimate=pl.CostEstimate(flops=2**20, bytes_accessed=3 * 2**19, transcendentals=2**16),
        name="finish",
    )(mine, other)


def base_term(blocks, other, tokens):
    weights = jnp.concatenate([blocks[:GROUPS], other[:GROUPS]], axis=1)
    weights = lax.all_to_all(weights, TENSOR, 0, 0, tiled=True)
    parts = project(weights, tokens)
    parts = lax.all_to_all(parts.reshape(GROUPS, TOKENS // GROUPS, -1), TENSOR, 0, 0, tiled=True)
    return tuple(add_up(parts))


def adapter_term(blocks, other, tokens):
    side = lax.all_to_all(shrink(other, blocks, tokens), TENSOR, 0, 0, tiled=True)
    shrunk = lax.all_to_all(copies_of(side, lax.axis_size("z")), "z", 0, 0, tiled=True)
    shrunk = lax.all_gather(shrunk, "xl", axis=0, tiled=True)
    return tuple(grow(side, shrunk))


def per_device(tokens, gate_ids, up_ids, gate_powers, up_powers, gate_b, up_b, gate_a, up_a):
    blocks = decode(gate_ids, up_ids, gate_powers, up_powers, gate_b, up_b, gate_a, up_a)
    swap = [(0, 1), (1, 0)]
    other = lax.ppermute(blocks, "c", swap)
    mine, theirs = lax.cond(lax.axis_index("c") == 0, base_term, adapter_term, blocks, other, tokens)
    return finish(mine, lax.ppermute(theirs, "c", swap))


def solution(mesh):
    split = Mesh(mesh.devices.reshape(2, 16, 2, 4, 2), ("xl", "z", "c", "y", "xh"))
    rows = P(FSDP + TENSOR, None)
    placed = (P(None, TENSOR), rows, rows, rows, rows, rows, rows, P(FSDP, TENSOR), P(FSDP, TENSOR))
    return jax.shard_map(per_device, mesh=split, in_specs=placed, out_specs=P(TENSOR, FSDP), check_vma=False)
```

time: 84.3 us -> 75.1 us (0.89)
  the two profiles are of different devices: /device:TPU:32 before, /device:TPU:1 now
where the time goes in v2:
time: 75.1 us; the launch traced here: 74.7 us
  blocking collectives  42 us (56%)
  starting transfers between devices  15.6 us (21%)
  Pallas kernels  12.1 us (16%)
  waiting for transfers between devices  3.89 us (5%)
  local copies, waits for them, and re-layouts  0.96 us (1%)
    all_to_all x1, blocking collectives, adapter_term(): lax.all_to_all(copies_of(side, lax.axis_size('z')), 'z', 0, 0, tiled=True)  24.4 us
    all_to_all x1, blocking collectives, adapter_term(): lax.all_to_all(shrink(other, blocks, tokens), TENSOR, 0, 0, tiled=True)  12.8 us
    ppermute x1, starting transfers between devices, per_device(): other = lax.ppermute(blocks, 'c', swap)  8.79 us
    ppermute x1, starting transfers between devices, per_device(): return finish(mine, lax.ppermute(theirs, 'c', swap))  6.86 us
    pallas_call x1, Pallas kernels, decode(): pl.pallas_call(decode_kernel, in_specs=[hbm] * 4 + [vmem] * 4, out_specs=...  6.12 us
    all_gather x1, blocking collectives, adapter_term(): shrunk = lax.all_gather(shrunk, 'xl', axis=0, tiled=True)  4.79 us
    ppermute x1, waiting for transfers between devices, per_device(): other = lax.ppermute(blocks, 'c', swap)  2.63 us
    pallas_call x1, Pallas kernels, shrink(): pl.pallas_call(shrink_kernel, grid=(1,), in_specs=[side, side, pl.BlockSp...  2.63 us
  transfers between devices with their start and end apart: 2, of which 2 were waited for; matrix products, arithmetic and copies ran while one was open for 0% of the time, Pallas kernels for 0%

profile of v2, /device:TPU:1, one launch (start us, length us, event | category | flops | bytes accessed | tf_op | source)
XLA Modules:
  0.0 74.7 jit_solution(11283388007582554006)
XLA Ops:
  0.0 6.1 %decode.1 = bf16[10,64,1024]{2,1,0:T(8,128)(2,1)S(1)} custom-call(s32[32,8192]{1,0:T(8,128)} %gate_ids.1, s32[32,8192]{1,0:T(8,128)} %up_ids.1, s32[32,128]{1,0:T(8,128)} %gate_powers.1, s32[32,128]{1,0:T(8,128)} %up_powers.1, bf16[32,128]{1,0:T(8,128)(2,1)} %gate_b.1, bf16[32,128]{1,0:T(8,128)(2,1)} %up_b.1, bf16[2,1024]{1,0:T(2,128)(2,1)} %gate_a.1, ...), custom_call_target="tpu_custom_call" | custom-call | flops 16777216 | bytes 3145728 | tf_op jit(solution)/shard_map/decode/pallas_call | solution.py:95
  6.1 8.8 %collective-permute-start = (bf16[10,64,1024]{2,1,0:T(8,128)(2,1)S(1)}, bf16[10,64,1024]{2,1,0:T(8,128)(2,1)S(1)}, u32[]{:S(2)}, u32[]{:S(2)}) collective-permute-start(bf16[10,64,1024]{2,1,0:T(8,128)(2,1)S(1)} %decode.1), channel_id=1, source_target_pairs={{0,8},{8,0},{1,9},{9,1},{2,10},{10,2},{3,11},{11,3},{4,12},{12,4},... | collective-permute-start | bytes 3932168 | tf_op jit(solution)/shard_map/ppermute | solution.py:285
  14.9 2.6 %collective-permute-done = bf16[10,64,1024]{2,1,0:T(8,128)(2,1)S(1)} collective-permute-done((bf16[10,64,1024]{2,1,0:T(8,128)(2,1)S(1)}, bf16[10,64,1024]{2,1,0:T(8,128)(2,1)S(1)}, u32[]{:S(2)}, u32[]{:S(2)}) %collective-permute-start) | collective-permute-done | bytes 1310752 | tf_op jit(solution)/shard_map/ppermute | solution.py:285
  17.6 48.3 %conditional.1 = ((f32[168,512]{1,0:T(8,128)S(1)}, f32[168,512]{1,0:T(8,128)S(1)})) conditional(s32[]{:T(128)} %convert_element_type.3, (bf16[1344,1024]{1,0:T(8,128)(2,1)}, bf16[10,64,1024]{2,1,0:T(8,128)(2,1)S(1)}, bf16[10,64,1024]{2,1,0:T(8,128)(2,1)S(1)}) %tuple.11, (bf16[10,64,1024]{2,1,0:T(8,128)(2,1)S(1)}, bf16[10,64,1024]{2,1,0:T(8,128)(2,1)S(1)}, ...), branch_computations={%region_0.0_spmd, %region_1.0_spmd} | conditional | flops 2824863744 | bytes 40632356 | solution.py:286
  17.6 2.6 %shrink.1 = bf16[8,144,128]{2,1,0:T(8,128)(2,1)S(1)} custom-call(bf16[10,64,1024]{2,1,0:T(8,128)(2,1)S(1)} %get-tuple-element.17.first, bf16[10,64,1024]{2,1,0:T(8,128)(2,1)S(1)} %get-tuple-element.18.second, bf16[8,168,1024]{2,1,0:T(8,128)(2,1)} %bitcast.3), custom_call_target="tpu_custom_call" | custom-call | flops 16777216 | bytes 3145728 | tf_op jit(solution)/shard_map/cond/branch_0_fun/shrink/pallas_call | solution.py:186
  20.2 12.8 %all_to_all.16.side = bf16[8,144,128]{2,1,0:T(8,128)(2,1)} all-to-all(bf16[8,144,128]{2,1,0:T(8,128)(2,1)S(1)} %shrink.1), channel_id=1, replica_groups=mesh['xl'=2,'z'=16,'c'=2,'y'=4,'xh'=2] {'y','xh'}, dimensions={0} | all-to-all | bytes 589824 | tf_op jit(solution)/shard_map/cond/branch_0_fun/all_to_all | solution.py:276
  33.0 1.6 %copies.1 = bf16[16,16,128]{2,1,0:T(8,128)(2,1)} custom-call(bf16[8,144,128]{2,1,0:T(8,128)(2,1)} %all_to_all.16.side), custom_call_target="tpu_custom_call" | custom-call | flops 16384 | bytes 524288 | tf_op jit(solution)/shard_map/cond/branch_0_fun/copies/pallas_call | solution.py:207
  34.6 24.4 %all_to_all.17 = bf16[16,16,128]{2,1,0:T(8,128)(2,1)S(1)} all-to-all(bf16[16,16,128]{2,1,0:T(8,128)(2,1)} %copies.1), channel_id=1, replica_groups=mesh['xl'=2,'z'=16,'c'=2,'y'=4,'xh'=2] {'z'}, dimensions={0} | all-to-all | bytes 131072 | tf_op jit(solution)/shard_map/cond/branch_0_fun/all_to_all | solution.py:277
  59.0 4.8 %all_gather.2.shrunk = bf16[32,16,128]{2,1,0:T(8,128)(2,1)S(1)} all-gather(bf16[16,16,128]{2,1,0:T(8,128)(2,1)S(1)} %all_to_all.17), channel_id=1, replica_groups=mesh['xl'=2,'z'=16,'c'=2,'y'=4,'xh'=2] {'xl'}, dimensions={0}, use_global_device_ids=true | all-gather | bytes 196608 | tf_op jit(solution)/shard_map/cond/branch_0_fun/all_gather | solution.py:278
  63.8 0.0 copy-start
  63.8 1.0 %copy-done = bf16[8,144,128]{2,1,0:T(8,128)(2,1)S(1)} copy-done((bf16[8,144,128]{2,1,0:T(8,128)(2,1)S(1)}, bf16[8,144,128]{2,1,0:T(8,128)(2,1)}, u32[]{:S(2)}) %copy-start) | copy-done | bytes 294936 | tf_op jit(solution)/shard_map/cond
  64.8 1.1 %grow.1 = (f32[168,512]{1,0:T(8,128)S(1)}, f32[168,512]{1,0:T(8,128)S(1)}) custom-call(bf16[8,144,128]{2,1,0:T(8,128)(2,1)S(1)} %copy-done, bf16[32,16,128]{2,1,0:T(8,128)(2,1)S(1)} %all_gather.2.shrunk), custom_call_target="tpu_custom_call" | custom-call | flops 33554432 | bytes 1048576 | tf_op jit(solution)/shard_map/cond/branch_0_fun/grow/pallas_call | solution.py:241
  65.8 6.9 %collective-permute-start.1 = (f32[168,512]{1,0:T(8,128)S(1)}, f32[168,512]{1,0:T(8,128)S(1)}, u32[]{:S(2)}, u32[]{:S(2)}) collective-permute-start(f32[168,512]{1,0:T(8,128)S(1)} %get-tuple-element.26), channel_id=1, source_target_pairs={{0,8},{8,0},{1,9},{9,1},{2,10},{10,2},{3,11},{11,3},{4,12},{12,4},... | collective-permute-start | bytes 1032200 | tf_op jit(solution)/shard_map/ppermute | solution.py:287
  72.7 1.3 %collective-permute-done.1.other = f32[168,512]{1,0:T(8,128)S(1)} collective-permute-done((f32[168,512]{1,0:T(8,128)S(1)}, f32[168,512]{1,0:T(8,128)S(1)}, u32[]{:S(2)}, u32[]{:S(2)}) %collective-permute-start.1) | collective-permute-done | bytes 344096 | tf_op jit(solution)/shard_map/ppermute | solution.py:287
  74.0 0.7 finish.1
Async XLA Ops:
  6.1 11.4 %collective-permute-start = (bf16[10,64,1024]{2,1,0:T(8,128)(2,1)S(1)}, bf16[10,64,1024]{2,1,0:T(8,128)(2,1)S(1)}, u32[]{:S(2)}, u32[]{:S(2)}) collective-permute-start(bf16[10,64,1024]{2,1,0:T(8,128)(2,1)S(1)} %decode.1), channel_id=1, source_target_pairs={{0,8},{8,0},{1,9},{9,1},{2,10},{10,2},{3,11},{11,3},{4,12},{12,4},... | collective-permute-start | bytes 3932168 | tf_op jit(solution)/shard_map/ppermute | solution.py:285
  63.8 1.0 %copy-start = (bf16[8,144,128]{2,1,0:T(8,128)(2,1)S(1)}, bf16[8,144,128]{2,1,0:T(8,128)(2,1)}, u32[]{:S(2)}) copy-start(bf16[8,144,128]{2,1,0:T(8,128)(2,1)} %all_to_all.16.side) | copy-start | bytes 884740 | tf_op jit(solution)/shard_map/cond
  65.8 8.1 %collective-permute-start.1 = (f32[168,512]{1,0:T(8,128)S(1)}, f32[168,512]{1,0:T(8,128)S(1)}, u32[]{:S(2)}, u32[]{:S(2)}) collective-permute-start(f32[168,512]{1,0:T(8,128)S(1)} %get-tuple-element.26), channel_id=1, source_target_pairs={{0,8},{8,0},{1,9},{9,1},{2,10},{10,2},{3,11},{11,3},{4,12},{12,4},... | collective-permute-start | bytes 1032200 | tf_op jit(solution)/shard_map/ppermute | solution.py:287

commit v3 on v2

--- a/solution.py
+++ b/solution.py
@@ -41,37 +41,38 @@
 TENSOR = ("y", "xh")
 def pick(ids, low, high):
     if high - low == 1:
-        return jnp.full(ids.shape, LEVELS[low], jnp.float32)
+        return jnp.full(ids.shape, LEVELS[low], jnp.bfloat16)
     middle = (low + high) // 2
-    return jnp.where(ids < middle, pick(ids, low, middle), pick(ids, middle, high))
+    return jnp.where(ids < jnp.int16(middle), pick(ids, low, middle), pick(ids, middle, high))
 
 
 def lookup(table, index):
     return jnp.take_along_axis(table, index, axis=1, mode="promise_in_bounds")
 
 
-def decode_kernel(gate_ids, up_ids, gate_powers, up_powers, gate_b, up_b, gate_a, up_a, out, ids, small, blocks, ready, near, sent):
-    extra = [
-        pltpu.make_async_copy(powers, small.at[p], near.at[p]) for p, powers in enumerate((gate_powers, up_powers))
-    ]
-    loads, stores = [], []
+def decode_kernel(gate_ids, up_ids, gate_powers, up_powers, gate_b, up_b, gate_a, up_a, out, ids, small, thin, blocks, ready, near, sent):
+    extra, stores = [], []
+    for p, (powers, factor, a) in enumerate(((gate_powers, gate_b, gate_a), (up_powers, up_b, up_a))):
+        extra.append(pltpu.make_async_copy(powers, small.at[p], near.at[p]))
+        extra.append(pltpu.make_async_copy(a, thin.at[p], near.at[2 + p]))
+        place = out.at[GROUPS, pl.ds(p * ROWS, ROWS), pl.ds(0, RANK)]
+        stores.append(pltpu.make_async_copy(factor, place, sent.at[GROUPS + 1 + p]))
+    loads = []
     for k in range(GROUPS):
         columns = pl.ds(k * WIDTH, WIDTH)
         loads.append(
             [pltpu.make_async_copy(ref.at[:, columns], ids.at[p, k], ready.at[p, k]) for p, ref in enumerate((gate_ids, up_ids))]
         )
-    for copy in extra + sum(loads, []):
+    for copy in extra + sum(loads, []) + stores:
         copy.start()
-    blocks[GROUPS, :, :] = jnp.zeros((2 * ROWS, WIDTH), jnp.bfloat16)
-    blocks[GROUPS, pl.ds(0, ROWS), pl.ds(0, RANK)] = gate_b[...]
-    blocks[GROUPS, pl.ds(ROWS, ROWS), pl.ds(0, RANK)] = up_b[...]
-    blocks[GROUPS + 1, :, :] = jnp.zeros((2 * ROWS, WIDTH), jnp.bfloat16)
-    blocks[GROUPS + 1, pl.ds(0, 2), :] = gate_a[...]
-    blocks[GROUPS + 1, pl.ds(2, 2), :] = up_a[...]
-    stores.append(pltpu.make_async_copy(blocks.at[pl.ds(GROUPS, 2)], out.at[pl.ds(GROUPS, 2)], sent.at[GROUPS]))
-    stores[-1].start()
     for copy in extra:
         copy.wait()
+    rows = jnp.concatenate([thin[0].astype(jnp.float32), thin[1].astype(jnp.float32), jnp.zeros((12, WIDTH), jnp.float32)], axis=0)
+    blocks[GROUPS, pl.ds(0, 16), :] = rows.astype(jnp.bfloat16)
+    stores.append(
+        pltpu.make_async_copy(blocks.at[GROUPS, pl.ds(0, 16)], out.at[GROUPS + 1, pl.ds(0, 16)], sent.at[GROUPS])
+    )
+    stores[-1].start()
     half = lax.broadcasted_iota(jnp.int32, (ROWS, LANES), 1) // BLOCK
     scales = [(jnp.int32(1) << (small[p] + 8)).astype(jnp.float32) * 2.0**-8 for p in range(2)]
     for k in range(GROUPS):
@@ -80,9 +81,9 @@
             rows = pl.ds(p * ROWS, ROWS)
             for chunk in range(WIDTH // LANES):
                 columns = pl.ds(chunk * LANES, LANES)
-                level = pick(ids[p, k, :, columns], 0, len(LEVELS))
+                level = pick(ids[p, k, :, columns].astype(jnp.int16), 0, len(LEVELS))
                 scale = lookup(scales[p], half + (k * (WIDTH // BLOCK) + chunk * (LANES // BLOCK)))
-                blocks[k, rows, columns] = (level * scale).astype(jnp.bfloat16)
+                blocks[k, rows, columns] = level * scale.astype(jnp.bfloat16)
         stores.append(pltpu.make_async_copy(blocks.at[k], out.at[k], sent.at[k]))
         stores[-1].start()
     for store in stores:
@@ -91,19 +92,20 @@
 
 def decode(*args):
     shape = (GROUPS + 2, 2 * ROWS, WIDTH)
-    hbm, vmem = pl.BlockSpec(memory_space=pltpu.HBM), pl.BlockSpec(memory_space=pltpu.VMEM)
+    hbm = pl.BlockSpec(memory_space=pltpu.HBM)
     return pl.pallas_call(
         decode_kernel,
-        in_specs=[hbm] * 4 + [vmem] * 4,
+        in_specs=[hbm] * 8,
         out_specs=hbm,
         out_shape=jax.ShapeDtypeStruct(shape, jnp.bfloat16),
         scratch_shapes=[
             pltpu.VMEM((2, GROUPS, ROWS, WIDTH), jnp.int32),
             pltpu.VMEM((2, ROWS, LANES), jnp.int32),
-            pltpu.VMEM(shape, jnp.bfloat16),
+            pltpu.VMEM((2, 2, WIDTH), jnp.bfloat16),
+            pltpu.VMEM((GROUPS + 1, 2 * ROWS, WIDTH), jnp.bfloat16),
             pltpu.SemaphoreType.DMA((2, GROUPS)),
-            pltpu.SemaphoreType.DMA((2,)),
-            pltpu.SemaphoreType.DMA((GROUPS + 1,)),
+            pltpu.SemaphoreType.DMA((4,)),
+            pltpu.SemaphoreType.DMA((GROUPS + 3,)),
         ],
         compiler_params=pltpu.CompilerParams(vmem_limit_bytes=62 * 2**20),
         cost_estimate=pl.CostEstimate(flops=2**24, bytes_accessed=3 * 2**20, transcendentals=0),
@@ -151,7 +153,7 @@
 
 def add_up_kernel(parts, mine, theirs):
     half = 2 * GROUPS * ROWS
-    for to, columns in ((mine, pl.ds(0, half)), (theirs, pl.ds(half, half))):
+    for to, columns in ((theirs, pl.ds(0, half)), (mine, pl.ds(half, half))):
         total = parts[0, :, columns].astype(jnp.float32)
         for k in range(1, GROUPS):
             total = total + parts[k, :, columns].astype(jnp.float32)
@@ -195,48 +197,62 @@
     )(first, second, tokens.reshape(GROUPS, TOKENS // GROUPS, WIDTH))
 
 
-def gather_kernel(side, out):
+def copies_kernel(side, out):
     total = side[0, pl.ds(4 * ROWS, 16), :].astype(jnp.float32)
     for k in range(1, GROUPS):
         total = total + side[k, pl.ds(4 * ROWS, 16), :].astype(jnp.float32)
-    for z in range(out.shape[0]):
-        out[z] = total.astype(jnp.bfloat16)
+    for place in range(out.shape[0]):
+        out[place] = total.astype(jnp.bfloat16)
 
 
 def copies_of(side, count):
     return pl.pallas_call(
-        gather_kernel,
+        copies_kernel,
         out_shape=jax.ShapeDtypeStruct((count, 16, LANES), jnp.bfloat16),
         cost_estimate=pl.CostEstimate(flops=2**14, bytes_accessed=2**19, transcendentals=0),
         name="copies",
     )(side)
 
 
-def grow_kernel(side, shrunk, mine, theirs):
-    count = TOKENS // GROUPS
+def spread_kernel(side, out):
     rank = lax.broadcasted_iota(jnp.int32, (RANK, 2 * RANK), 0)
     place = lax.broadcasted_iota(jnp.int32, (RANK, 2 * RANK), 1)
-    spreads = [
-        ((place % 4 // 2 == p) & (place // 4 * 2 + place % 2 == rank)).astype(jnp.float32).astype(jnp.bfloat16) for p in range(2)
-    ]
+    for q in range(4):
+        hit = (place % 4 // 2 == q % 2) & (place // 4 * 2 + place % 2 == rank)
+        factor = side[:, pl.ds(q * ROWS, ROWS), :].reshape(GROUPS * ROWS, RANK)
+        out[q] = jnp.dot(
+            factor, hit.astype(jnp.float32).astype(jnp.bfloat16), preferred_element_type=jnp.float32
+        ).astype(jnp.bfloat16)
+
+
+def spread_out(side):
+    return pl.pallas_call(
+        spread_kernel,
+        out_shape=jax.ShapeDtypeStruct((4, GROUPS * ROWS, 2 * RANK), jnp.bfloat16),
+        compiler_params=pltpu.CompilerParams(vmem_limit_bytes=16 * 2**20),
+        cost_estimate=pl.CostEstimate(flops=2**26, bytes_accessed=2**20, transcendentals=0),
+        name="spread_out",
+    )(side)
+
+
+def grow_kernel(factors, shrunk, mine, theirs):
+    count = TOKENS // GROUPS
     values = shrunk[...].astype(jnp.float32)
     low = values[:, 0:8, :].reshape(2 * RANK, LANES).T.astype(jnp.bfloat16)
     high = values[:, 8:16, :].reshape(2 * RANK, LANES).T.astype(jnp.bfloat16)
     half = GROUPS * ROWS
     for q in range(4):
-        factor = side[:, pl.ds(q * ROWS, ROWS), :].reshape(half, RANK)
-        factor = jnp.dot(factor, spreads[q % 2], preferred_element_type=jnp.float32).astype(jnp.bfloat16)
-        to = theirs if q < 2 else mine
+        to = mine if q < 2 else theirs
         columns = pl.ds(q % 2 * half, half)
         to[pl.ds(0, LANES), columns] = lax.dot_general(
-            low, factor, (((1,), (1,)), ((), ())), preferred_element_type=jnp.float32
+            low, factors[q], (((1,), (1,)), ((), ())), preferred_element_type=jnp.float32
         )
         to[pl.ds(LANES, count - LANES), columns] = lax.dot_general(
-            high, factor, (((1,), (1,)), ((), ())), preferred_element_type=jnp.float32
+            high, factors[q], (((1,), (1,)), ((), ())), preferred_element_type=jnp.float32
         )[: count - LANES]
 
 
-def grow(side, shrunk):
+def grow(factors, shrunk):
     shape = jax.ShapeDtypeStruct((TOKENS // GROUPS, 2 * GROUPS * ROWS), jnp.float32)
     return pl.pallas_call(
         grow_kernel,
@@ -244,28 +260,32 @@
         compiler_params=pltpu.CompilerParams(vmem_limit_bytes=32 * 2**20),
         cost_estimate=pl.CostEstimate(flops=2**25, bytes_accessed=2**20, transcendentals=0),
         name="grow",
-    )(side, shrunk)
-
-
-def finish_kernel(mine, other, out):
+    )(factors, shrunk)
+
+
+def finish_kernel(core, mine, both, out):
     half = GROUPS * ROWS
+    other = both.at[1 - core[0]]
     gate = mine[:, :half] + other[:, :half]
     up = mine[:, half:] + other[:, half:]
     out[...] = (gate / (1.0 + jnp.exp(-gate)) * up).astype(jnp.bfloat16)
 
 
-def finish(mine, other):
+def finish(core, mine, both):
+    vmem = pl.BlockSpec(memory_space=pltpu.VMEM)
     return pl.pallas_call(
         finish_kernel,
+        in_specs=[pl.BlockSpec(memory_space=pltpu.SMEM), vmem, vmem],
+        out_specs=vmem,
         out_shape=jax.ShapeDtypeStruct((TOKENS // GROUPS, GROUPS * ROWS), jnp.bfloat16),
         compiler_params=pltpu.CompilerParams(vmem_limit_bytes=32 * 2**20),
         cost_estimate=pl.CostEstimate(flops=2**20, bytes_accessed=3 * 2**19, transcendentals=2**16),
         name="finish",
-    )(mine, other)
+    )(core, mine, both)
 
 
 def base_term(blocks, other, tokens):
-    weights = jnp.concatenate([blocks[:GROUPS], other[:GROUPS]], axis=1)
+    weights = jnp.concatenate([other[:GROUPS], blocks[:GROUPS]], axis=1)
     weights = lax.all_to_all(weights, TENSOR, 0, 0, tiled=True)
     parts = project(weights, tokens)
     parts = lax.all_to_all(parts.reshape(GROUPS, TOKENS // GROUPS, -1), TENSOR, 0, 0, tiled=True)
@@ -273,18 +293,18 @@
 
 
 def adapter_term(blocks, other, tokens):
-    side = lax.all_to_all(shrink(other, blocks, tokens), TENSOR, 0, 0, tiled=True)
-    shrunk = lax.all_to_all(copies_of(side, lax.axis_size("z")), "z", 0, 0, tiled=True)
-    shrunk = lax.all_gather(shrunk, "xl", axis=0, tiled=True)
-    return tuple(grow(side, shrunk))
+    side = lax.all_to_all(shrink(blocks, other, tokens), TENSOR, 0, 0, tiled=True)
+    copies = copies_of(side, lax.axis_size("xl") * lax.axis_size("z"))
+    shrunk = lax.all_to_all(copies, ("xl", "z"), 0, 0, tiled=True)
+    return tuple(grow(spread_out(side), shrunk))
 
 
 def per_device(tokens, gate_ids, up_ids, gate_powers, up_powers, gate_b, up_b, gate_a, up_a):
+    core = lax.axis_index("c").astype(jnp.int32)
     blocks = decode(gate_ids, up_ids, gate_powers, up_powers, gate_b, up_b, gate_a, up_a)
-    swap = [(0, 1), (1, 0)]
-    other = lax.ppermute(blocks, "c", swap)
-    mine, theirs = lax.cond(lax.axis_index("c") == 0, base_term, adapter_term, blocks, other, tokens)
-    return finish(mine, lax.ppermute(theirs, "c", swap))
+    other = lax.ppermute(blocks, "c", [(0, 1), (1, 0)])
+    mine, theirs = lax.cond(core == 0, adapter_term, base_term, blocks, other, tokens)
+    return finish(core.reshape(1), mine, lax.all_gather(theirs, "c", axis=0))
 
 
 def solution(mesh):

time: 75.1 us -> 70 us (0.932)
  starting transfers between devices: 15.6 us -> 8.79 us
  blocking collectives: 42 us -> 48.3 us
  Pallas kernels: 12.1 us -> 9.53 us
  waiting for transfers between devices: 3.89 us -> 2.63 us
  local copies, waits for them, and re-layouts: 0.96 us -> 0.18 us
    all_to_all x2, blocking collectives: 37.2 us -> 46 us  [the longest x1 24.2 us: base_term(): lax.all_to_all(parts.reshape(GROUPS, TOKENS // GROUPS, -1), TENSOR, 0, 0,...]
    ppermute x2 -> x1, starting transfers between devices: 15.6 us -> 8.79 us  [per_device(): other = lax.ppermute(blocks, 'c', [(0, 1), (1, 0)])]
    pallas_call x5 -> x4, Pallas kernels: 12.1 us -> 9.53 us  [the longest x1 4.73 us: decode(): pl.pallas_call(decode_kernel, in_specs=[hbm] * 8, out_specs=hbm, out_shap...]
    all_gather x1, blocking collectives: 4.79 us -> 2.3 us  [per_device(): return finish(core.reshape(1), mine, lax.all_gather(theirs, 'c', axis=0))]
    ppermute x2 -> x1, waiting for transfers between devices: 3.89 us -> 2.63 us  [per_device(): other = lax.ppermute(blocks, 'c', [(0, 1), (1, 0)])]
    cond x2, local copies, waits for them, and re-layouts: 0.96 us -> 0.01 us
  transfers between devices with their start and end apart: 2 -> 1, of which waited for: 2 -> 1; matrix products, arithmetic and copies ran while one was open for 0% -> 0% of each run, Pallas kernels for 0% -> 0%
where the time goes in v3:
time: 70 us; the launch traced here: 69.7 us
  blocking collectives  48.3 us (69%)
  Pallas kernels  9.53 us (14%)
  starting transfers between devices  8.79 us (13%)
  waiting for transfers between devices  2.63 us (4%)
    all_to_all x1, blocking collectives, base_term(): lax.all_to_all(parts.reshape(GROUPS, TOKENS // GROUPS, -1), TENSOR, 0, 0,...  24.2 us
    all_to_all x1, blocking collectives, base_term(): weights = lax.all_to_all(weights, TENSOR, 0, 0, tiled=True)  21.8 us
    ppermute x1, starting transfers between devices, per_device(): other = lax.ppermute(blocks, 'c', [(0, 1), (1, 0)])  8.79 us
    pallas_call x1, Pallas kernels, decode(): pl.pallas_call(decode_kernel, in_specs=[hbm] * 8, out_specs=hbm, out_shap...  4.73 us
    pallas_call x1, Pallas kernels, project(): pl.pallas_call(project_kernel, in_specs=[place, pl.BlockSpec(memory_space...  3.75 us
    ppermute x1, waiting for transfers between devices, per_device(): other = lax.ppermute(blocks, 'c', [(0, 1), (1, 0)])  2.63 us
    all_gather x1, blocking collectives, per_device(): return finish(core.reshape(1), mine, lax.all_gather(theirs, 'c', axis=0))  2.3 us
  transfers between devices with their start and end apart: 1, of which 1 were waited for; matrix products, arithmetic and copies ran while one was open for 0% of the time, Pallas kernels for 0%

profile of v3, /device:TPU:1, one launch (start us, length us, event | category | flops | bytes accessed | tf_op | source)
XLA Modules:
  0.0 69.7 jit_solution(11398995732114451339)
XLA Ops:
  0.0 4.7 %decode.1 = bf16[10,64,1024]{2,1,0:T(8,128)(2,1)S(1)} custom-call(s32[32,8192]{1,0:T(8,128)} %gate_ids.1, s32[32,8192]{1,0:T(8,128)} %up_ids.1, s32[32,128]{1,0:T(8,128)} %gate_powers.1, s32[32,128]{1,0:T(8,128)} %up_powers.1, bf16[32,128]{1,0:T(8,128)(2,1)} %gate_b.1, bf16[32,128]{1,0:T(8,128)(2,1)} %up_b.1, bf16[2,1024]{1,0:T(2,128)(2,1)} %gate_a.1, ...), custom_call_target="tpu_custom_call" | custom-call | flops 16777216 | bytes 3145728 | tf_op jit(solution)/shard_map/decode/pallas_call | solution.py:96
  4.7 8.8 %collective-permute-start = (bf16[10,64,1024]{2,1,0:T(8,128)(2,1)S(1)}, bf16[10,64,1024]{2,1,0:T(8,128)(2,1)S(1)}, u32[]{:S(2)}, u32[]{:S(2)}) collective-permute-start(bf16[10,64,1024]{2,1,0:T(8,128)(2,1)S(1)} %decode.1), channel_id=1, source_target_pairs={{0,8},{8,0},{1,9},{9,1},{2,10},{10,2},{3,11},{11,3},{4,12},{12,4},... | collective-permute-start | bytes 3932168 | tf_op jit(solution)/shard_map/ppermute | solution.py:305
  13.5 2.6 %collective-permute-done = bf16[10,64,1024]{2,1,0:T(8,128)(2,1)S(1)} collective-permute-done((bf16[10,64,1024]{2,1,0:T(8,128)(2,1)S(1)}, bf16[10,64,1024]{2,1,0:T(8,128)(2,1)S(1)}, u32[]{:S(2)}, u32[]{:S(2)}) %collective-permute-start) | collective-permute-done | bytes 1310752 | tf_op jit(solution)/shard_map/ppermute | solution.py:305
  16.2 50.5 %conditional.1 = ((f32[168,512]{1,0:T(8,128)S(1)}, f32[168,512]{1,0:T(8,128)S(1)})) conditional(s32[]{:T(128)} %convert_element_type.3, (bf16[10,64,1024]{2,1,0:T(8,128)(2,1)S(1)}, bf16[10,64,1024]{2,1,0:T(8,128)(2,1)S(1)}, bf16[1344,1024]{1,0:T(8,128)(2,1)}) %tuple.11, (bf16[1344,1024]{1,0:T(8,128)(2,1)}, bf16[10,64,1024]{2,1,0:T(8,128)(2,1)S(1)}, ...), branch_computations={%region_0.0_spmd, %region_1.0_spmd} | conditional | flops 2824863744 | bytes 40632356 | solution.py:306
  16.2 0.1 slice.4
  16.3 0.1 slice.5
  16.4 0.2 pad_maximum_fusion
  16.5 0.0 copy-start.1
  16.6 21.8 %all_to_all.16.weights = bf16[8,128,1024]{2,1,0:T(8,128)(2,1)S(1)} all-to-all(bf16[8,128,1024]{2,1,0:T(8,128)(2,1)S(1)} %pad_maximum_fusion), channel_id=1, replica_groups=mesh['xl'=2,'z'=16,'c'=2,'y'=4,'xh'=2] {'y','xh'}, dimensions={0} | all-to-all | bytes 4194304 | tf_op jit(solution)/shard_map/cond/branch_0_fun/all_to_all | solution.py:289
  38.3 0.0 copy-done.1
  38.3 3.8 %project.1 = bf16[1344,1024]{1,0:T(8,128)(2,1)S(1)} custom-call(bf16[8,128,1024]{2,1,0:T(8,128)(2,1)S(1)} %all_to_all.16.weights, bf16[1344,1024]{1,0:T(8,128)(2,1)S(1)} %copy-done.1), custom_call_target="tpu_custom_call" | custom-call | flops 2818572288 | bytes 8388608 | tf_op jit(solution)/shard_map/cond/branch_0_fun/project/pallas_call | solution.py:138
  42.1 24.2 %all_to_all.17.parts = bf16[8,168,1024]{2,1,0:T(8,128)(2,1)S(1)} all-to-all(bf16[8,168,1024]{2,1,0:T(8,128)(2,1)S(1)} %bitcast.4), channel_id=1, replica_groups=mesh['xl'=2,'z'=16,'c'=2,'y'=4,'xh'=2] {'y','xh'}, dimensions={0} | all-to-all | bytes 5505024 | tf_op jit(solution)/shard_map/cond/branch_0_fun/all_to_all | solution.py:291
  66.3 0.3 add_up.1
  66.7 2.3 %all-gather = f32[336,512]{1,0:T(8,128)S(1)} all-gather(f32[168,512]{1,0:T(8,128)S(1)} %get-tuple-element.26), channel_id=2, replica_groups=mesh['xl'=2,'z'=16,'c'=2,'y'=4,'xh'=2] {'c'}, dimensions={0}, use_global_device_ids=true | all-gather | bytes 1032192 | tf_op jit(solution)/shard_map/all_gather | solution.py:307
  69.0 0.7 %finish.1 = bf16[168,256]{1,0:T(8,128)(2,1)} custom-call(s32[1]{0:T(128)} %bitcast.2.core, f32[168,512]{1,0:T(8,128)S(1)} %get-tuple-element.25.mine, f32[2,168,512]{2,1,0:T(8,128)S(1)} %bitcast.5), custom_call_target="tpu_custom_call" | custom-call | flops 1048576 | bytes 1572864 | tf_op jit(solution)/shard_map/finish/pallas_call | solution.py:276
Async XLA Ops:
  4.7 11.4 %collective-permute-start = (bf16[10,64,1024]{2,1,0:T(8,128)(2,1)S(1)}, bf16[10,64,1024]{2,1,0:T(8,128)(2,1)S(1)}, u32[]{:S(2)}, u32[]{:S(2)}) collective-permute-start(bf16[10,64,1024]{2,1,0:T(8,128)(2,1)S(1)} %decode.1), channel_id=1, source_target_pairs={{0,8},{8,0},{1,9},{9,1},{2,10},{10,2},{3,11},{11,3},{4,12},{12,4},... | collective-permute-start | bytes 3932168 | tf_op jit(solution)/shard_map/ppermute | solution.py:305
  16.5 21.8 %copy-start.1 = (bf16[1344,1024]{1,0:T(8,128)(2,1)S(1)}, bf16[1344,1024]{1,0:T(8,128)(2,1)}, u32[]{:S(2)}) copy-start(bf16[1344,1024]{1,0:T(8,128)(2,1)} %get-tuple-element.19.tokens) | copy-start | bytes 8257540 | tf_op jit(solution)/shard_map/cond

commit v4 on v3

--- a/solution.py
+++ b/solution.py
@@ -14,6 +14,7 @@
 WIDTH = 1024
 TOKENS = 1344
 LANES = 128
+PAIRS = 4
 PIECES = 2
 SIDE = 144
 
@@ -50,16 +51,18 @@
     return jnp.take_along_axis(table, index, axis=1, mode="promise_in_bounds")
 
 
-def decode_kernel(gate_ids, up_ids, gate_powers, up_powers, gate_b, up_b, gate_a, up_a, out, ids, small, thin, blocks, ready, near, sent):
+def decode_kernel(own, gate_ids, up_ids, gate_powers, up_powers, gate_b, up_b, gate_a, up_a, out, ids, small, thin, blocks, ready, near, sent):
     extra, stores = [], []
     for p, (powers, factor, a) in enumerate(((gate_powers, gate_b, gate_a), (up_powers, up_b, up_a))):
         extra.append(pltpu.make_async_copy(powers, small.at[p], near.at[p]))
         extra.append(pltpu.make_async_copy(a, thin.at[p], near.at[2 + p]))
-        place = out.at[GROUPS, pl.ds(p * ROWS, ROWS), pl.ds(0, RANK)]
-        stores.append(pltpu.make_async_copy(factor, place, sent.at[GROUPS + 1 + p]))
-    loads = []
+        place = out.at[PAIRS, pl.ds(p * ROWS, ROWS), pl.ds(0, RANK)]
+        stores.append(pltpu.make_async_copy(factor, place, sent.at[PAIRS + 1 + p]))
+    loads, groups = [], []
     for k in range(GROUPS):
-        columns = pl.ds(k * WIDTH, WIDTH)
+        group = k // 2 * 2 + (own[0] + k % 2) % 2
+        groups.append(group)
+        columns = pl.ds(pl.multiple_of(group * WIDTH, WIDTH), WIDTH)
         loads.append(
             [pltpu.make_async_copy(ref.at[:, columns], ids.at[p, k], ready.at[p, k]) for p, ref in enumerate((gate_ids, up_ids))]
         )
@@ -68,9 +71,11 @@
     for copy in extra:
         copy.wait()
     rows = jnp.concatenate([thin[0].astype(jnp.float32), thin[1].astype(jnp.float32), jnp.zeros((12, WIDTH), jnp.float32)], axis=0)
-    blocks[GROUPS, pl.ds(0, 16), :] = rows.astype(jnp.bfloat16)
+    blocks[PAIRS, pl.ds(0, 16), pl.ds(0, WIDTH)] = rows.astype(jnp.bfloat16)
     stores.append(
-        pltpu.make_async_copy(blocks.at[GROUPS, pl.ds(0, 16)], out.at[GROUPS + 1, pl.ds(0, 16)], sent.at[GROUPS])
+        pltpu.make_async_copy(
+            blocks.at[PAIRS, pl.ds(0, 16), pl.ds(0, WIDTH)], out.at[PAIRS, pl.ds(0, 16), pl.ds(WIDTH, WIDTH)], sent.at[PAIRS]
+        )
     )
     stores[-1].start()
     half = lax.broadcasted_iota(jnp.int32, (ROWS, LANES), 1) // BLOCK
@@ -80,32 +85,33 @@
             loads[k][p].wait()
             rows = pl.ds(p * ROWS, ROWS)
             for chunk in range(WIDTH // LANES):
-                columns = pl.ds(chunk * LANES, LANES)
-                level = pick(ids[p, k, :, columns].astype(jnp.int16), 0, len(LEVELS))
-                scale = lookup(scales[p], half + (k * (WIDTH // BLOCK) + chunk * (LANES // BLOCK)))
-                blocks[k, rows, columns] = level * scale.astype(jnp.bfloat16)
-        stores.append(pltpu.make_async_copy(blocks.at[k], out.at[k], sent.at[k]))
-        stores[-1].start()
+                level = pick(ids[p, k, :, pl.ds(chunk * LANES, LANES)].astype(jnp.int16), 0, len(LEVELS))
+                scale = lookup(scales[p], half + (groups[k] * (WIDTH // BLOCK) + chunk * (LANES // BLOCK)))
+                columns = pl.ds(k % 2 * WIDTH + chunk * LANES, LANES)
+                blocks[k // 2, rows, columns] = level * scale.astype(jnp.bfloat16)
+        if k % 2:
+            stores.append(pltpu.make_async_copy(blocks.at[k // 2], out.at[k // 2], sent.at[k // 2]))
+            stores[-1].start()
     for store in stores:
         store.wait()
 
 
 def decode(*args):
-    shape = (GROUPS + 2, 2 * ROWS, WIDTH)
+    shape = (PAIRS + 1, 2 * ROWS, 2 * WIDTH)
     hbm = pl.BlockSpec(memory_space=pltpu.HBM)
     return pl.pallas_call(
         decode_kernel,
-        in_specs=[hbm] * 8,
+        in_specs=[pl.BlockSpec(memory_space=pltpu.SMEM)] + [hbm] * 8,
         out_specs=hbm,
         out_shape=jax.ShapeDtypeStruct(shape, jnp.bfloat16),
         scratch_shapes=[
             pltpu.VMEM((2, GROUPS, ROWS, WIDTH), jnp.int32),
             pltpu.VMEM((2, ROWS, LANES), jnp.int32),
             pltpu.VMEM((2, 2, WIDTH), jnp.bfloat16),
-            pltpu.VMEM((GROUPS + 1, 2 * ROWS, WIDTH), jnp.bfloat16),
+            pltpu.VMEM(shape, jnp.bfloat16),
             pltpu.SemaphoreType.DMA((2, GROUPS)),
             pltpu.SemaphoreType.DMA((4,)),
-            pltpu.SemaphoreType.DMA((GROUPS + 3,)),
+            pltpu.SemaphoreType.DMA((PAIRS + 3,)),
         ],
         compiler_params=pltpu.CompilerParams(vmem_limit_bytes=62 * 2**20),
         cost_estimate=pl.CostEstimate(flops=2**24, bytes_accessed=3 * 2**20, transcendentals=0),
@@ -113,55 +119,76 @@
     )(*args)
 
 
-def project_kernel(weights, tokens, out, merged, held, ready):
+DIMS = (((1,), (1,)), ((), ()))
+
+
+def project_own_kernel(weights, tokens, out, rest, merged):
+    part = PAIRS * ROWS
+    for q in range(4):
+        merged[pl.ds(q * part, part), :] = weights[:, pl.ds(q * ROWS, ROWS), pl.ds(0, WIDTH)].reshape(part, WIDTH)
+        rest[pl.ds(q * part, part), :] = weights[:, pl.ds(q * ROWS, ROWS), pl.ds(WIDTH, WIDTH)].reshape(part, WIDTH)
+    out[...] = lax.dot_general(tokens[...], merged[...], DIMS, preferred_element_type=jnp.float32)
+
+
+def project_own(weights, tokens):
+    place = pl.BlockSpec(memory_space=pltpu.VMEM)
+    columns = 4 * PAIRS * ROWS
+    return pl.pallas_call(
+        project_own_kernel,
+        in_specs=[place, place],
+        out_specs=[place, place],
+        out_shape=[
+            jax.ShapeDtypeStruct((TOKENS, columns), jnp.float32),
+            jax.ShapeDtypeStruct((columns, WIDTH), jnp.bfloat16),
+        ],
+        scratch_shapes=[pltpu.VMEM((columns, WIDTH), jnp.bfloat16)],
+        compiler_params=pltpu.CompilerParams(vmem_limit_bytes=32 * 2**20),
+        cost_estimate=pl.CostEstimate(flops=TOKENS * 1024 * 1024, bytes_accessed=8 * 2**20, transcendentals=0),
+        name="project_own",
+    )(weights, tokens)
+
+
+def project_near_kernel(total, weights, tokens, out, held, ready):
     part = TOKENS // PIECES
     loads = []
     for i in range(PIECES):
-        loads.append(pltpu.make_async_copy(tokens.at[pl.ds(i * part, part)], held.at[pl.ds(i * part, part)], ready.at[i]))
+        rows = pl.ds(i * part, part)
+        loads.append(pltpu.make_async_copy(tokens.at[rows], held.at[rows], ready.at[i]))
         loads[-1].start()
-    half = GROUPS * ROWS
-    for q in range(4):
-        merged[pl.ds(q * half, half), :] = weights[:, pl.ds(q * ROWS, ROWS), :].reshape(half, WIDTH)
     for i in range(PIECES):
         rows = pl.ds(i * part, part)
         loads[i].wait()
+        product = lax.dot_general(held[rows, :], weights[...], DIMS, preferred_element_type=jnp.float32)
+        out[rows, :] = (total[rows, :] + product).astype(jnp.bfloat16)
+
+
+def project_near(total, weights, tokens):
+    place = pl.BlockSpec(memory_space=pltpu.VMEM)
+    return pl.pallas_call(
+        project_near_kernel,
+        in_specs=[place, place, pl.BlockSpec(memory_space=pltpu.HBM)],
+        out_specs=place,
+        out_shape=jax.ShapeDtypeStruct(total.shape, jnp.bfloat16),
+        scratch_shapes=[pltpu.VMEM((TOKENS, WIDTH), jnp.bfloat16), pltpu.SemaphoreType.DMA((PIECES,))],
+        compiler_params=pltpu.CompilerParams(vmem_limit_bytes=32 * 2**20),
+        cost_estimate=pl.CostEstimate(flops=TOKENS * 1024 * 1024, bytes_accessed=8 * 2**20, transcendentals=0),
+        name="project_near",
+    )(total, weights, tokens)
+
+
+def add_up_kernel(parts, mine, theirs):
+    part = PAIRS * ROWS
+    for x in range(2):
+        total = parts[x].astype(jnp.float32)
+        for y in range(1, PAIRS):
+            total = total + parts[2 * y + x].astype(jnp.float32)
         for q in range(4):
-            columns = pl.ds(q * half, half)
-            out[rows, columns] = lax.dot_general(
-                held[rows, :], merged[columns, :], (((1,), (1,)), ((), ())), preferred_element_type=jnp.float32
-            ).astype(jnp.bfloat16)
-
-
-def project(weights, tokens):
-    place = pl.BlockSpec(memory_space=pltpu.VMEM)
-    columns = 4 * GROUPS * ROWS
-    return pl.pallas_call(
-        project_kernel,
-        in_specs=[place, pl.BlockSpec(memory_space=pltpu.HBM)],
-        out_specs=place,
-        out_shape=jax.ShapeDtypeStruct((TOKENS, columns), jnp.bfloat16),
-        scratch_shapes=[
-            pltpu.VMEM((columns, WIDTH), jnp.bfloat16),
-            pltpu.VMEM((TOKENS, WIDTH), jnp.bfloat16),
-            pltpu.SemaphoreType.DMA((PIECES,)),
-        ],
-        compiler_params=pltpu.CompilerParams(vmem_limit_bytes=40 * 2**20),
-        cost_estimate=pl.CostEstimate(flops=2 * TOKENS * 1024 * 1024, bytes_accessed=8 * 2**20, transcendentals=0),
-        name="project",
-    )(weights, tokens)
-
-
-def add_up_kernel(parts, mine, theirs):
-    half = 2 * GROUPS * ROWS
-    for to, columns in ((theirs, pl.ds(0, half)), (mine, pl.ds(half, half))):
-        total = parts[0, :, columns].astype(jnp.float32)
-        for k in range(1, GROUPS):
-            total = total + parts[k, :, columns].astype(jnp.float32)
-        to[...] = total
+            to = theirs if q < 2 else mine
+            to[:, pl.ds((q % 2 * 2 + x) * part, part)] = total[:, q * part : (q + 1) * part]
 
 
 def add_up(parts):
-    shape = jax.ShapeDtypeStruct((parts.shape[1], parts.shape[2] // 2), jnp.float32)
+    shape = jax.ShapeDtypeStruct((parts.shape[1], parts.shape[2]), jnp.float32)
     return pl.pallas_call(
         add_up_kernel,
         out_shape=[shape, shape],
@@ -172,8 +199,8 @@
 
 
 def shrink_kernel(first, second, tokens, out):
-    a = jnp.concatenate([first[1, pl.ds(0, 4), :].astype(jnp.float32), second[1, pl.ds(0, 4), :].astype(jnp.float32)], axis=0)
-    a = a.astype(jnp.bfloat16)
+    a = [block[0, pl.ds(0, 16), pl.ds(WIDTH, WIDTH)].astype(jnp.float32)[0:4] for block in (first, second)]
+    a = jnp.concatenate(a, axis=0).astype(jnp.bfloat16)
     count = TOKENS // GROUPS
     for k in range(GROUPS):
         out[k, pl.ds(0, 2 * ROWS), :] = first[0, :, pl.ds(0, RANK)]
@@ -184,7 +211,7 @@
 
 
 def shrink(first, second, tokens):
-    side = pl.BlockSpec((2, 2 * ROWS, WIDTH), lambda i: (GROUPS // 2, 0, 0))
+    side = pl.BlockSpec((1, 2 * ROWS, 2 * WIDTH), lambda i: (PAIRS, 0, 0))
     return pl.pallas_call(
         shrink_kernel,
         grid=(1,),
@@ -219,7 +246,7 @@
     place = lax.broadcasted_iota(jnp.int32, (RANK, 2 * RANK), 1)
     for q in range(4):
         hit = (place % 4 // 2 == q % 2) & (place // 4 * 2 + place % 2 == rank)
-        factor = side[:, pl.ds(q * ROWS, ROWS), :].reshape(GROUPS * ROWS, RANK)
+        factor = jnp.concatenate([side[k, pl.ds(q * ROWS, ROWS), :] for k in (0, 2, 4, 6, 1, 3, 5, 7)], axis=0)
         out[q] = jnp.dot(
             factor, hit.astype(jnp.float32).astype(jnp.bfloat16), preferred_element_type=jnp.float32
         ).astype(jnp.bfloat16)
@@ -268,7 +295,13 @@
     other = both.at[1 - core[0]]
     gate = mine[:, :half] + other[:, :half]
     up = mine[:, half:] + other[:, half:]
-    out[...] = (gate / (1.0 + jnp.exp(-gate)) * up).astype(jnp.bfloat16)
+    result = (gate / (1.0 + jnp.exp(-gate)) * up).astype(jnp.bfloat16)
+    place = lax.broadcasted_iota(jnp.int32, (half, half), 0)
+    column = lax.broadcasted_iota(jnp.int32, (half, half), 1)
+    group = column // ROWS
+    wanted = (group % 2 * PAIRS + group // 2) * ROWS + column % ROWS
+    move = (place == wanted).astype(jnp.float32).astype(jnp.bfloat16)
+    out[...] = jnp.dot(result, move, preferred_element_type=jnp.float32).astype(jnp.bfloat16)
 
 
 def finish(core, mine, both):
@@ -284,16 +317,25 @@
     )(core, mine, both)
 
 
-def base_term(blocks, other, tokens):
-    weights = jnp.concatenate([other[:GROUPS], blocks[:GROUPS]], axis=1)
-    weights = lax.all_to_all(weights, TENSOR, 0, 0, tiled=True)
-    parts = project(weights, tokens)
+def exchange_weights(blocks, other, tokens):
+    weights = jnp.concatenate([other[:PAIRS], blocks[:PAIRS]], axis=1)
+    weights = lax.all_to_all(weights, "y", 0, 0, tiled=True)
+    return *project_own(weights, tokens), jnp.zeros((GROUPS, SIDE, LANES), jnp.bfloat16)
+
+
+def exchange_shrunk(blocks, other, tokens):
+    side = lax.all_to_all(shrink(blocks, other, tokens), TENSOR, 0, 0, tiled=True)
+    columns = 4 * PAIRS * ROWS
+    return jnp.zeros((TOKENS, columns), jnp.float32), jnp.zeros((columns, WIDTH), jnp.bfloat16), side
+
+
+def base_term(total, weights, side, near_tokens):
+    parts = project_near(total, weights, near_tokens)
     parts = lax.all_to_all(parts.reshape(GROUPS, TOKENS // GROUPS, -1), TENSOR, 0, 0, tiled=True)
     return tuple(add_up(parts))
 
 
-def adapter_term(blocks, other, tokens):
-    side = lax.all_to_all(shrink(blocks, other, tokens), TENSOR, 0, 0, tiled=True)
+def adapter_term(total, weights, side, near_tokens):
     copies = copies_of(side, lax.axis_size("xl") * lax.axis_size("z"))
     shrunk = lax.all_to_all(copies, ("xl", "z"), 0, 0, tiled=True)
     return tuple(grow(spread_out(side), shrunk))
@@ -301,9 +343,13 @@
 
 def per_device(tokens, gate_ids, up_ids, gate_powers, up_powers, gate_b, up_b, gate_a, up_a):
     core = lax.axis_index("c").astype(jnp.int32)
-    blocks = decode(gate_ids, up_ids, gate_powers, up_powers, gate_b, up_b, gate_a, up_a)
+    pairs = [(xl * 4 + 2 + xh, (1 - xl) * 4 + 2 + 1 - xh) for xl in range(2) for xh in range(2)]
+    near_tokens = lax.ppermute(tokens, ("xl", "c", "xh"), pairs)
+    own = lax.axis_index("xh").astype(jnp.int32).reshape(1)
+    blocks = decode(own, gate_ids, up_ids, gate_powers, up_powers, gate_b, up_b, gate_a, up_a)
     other = lax.ppermute(blocks, "c", [(0, 1), (1, 0)])
-    mine, theirs = lax.cond(core == 0, adapter_term, base_term, blocks, other, tokens)
+    total, weights, side = lax.cond(core == 0, exchange_shrunk, exchange_weights, blocks, other, tokens)
+    mine, theirs = lax.cond(core == 0, adapter_term, base_term, total, weights, side, near_tokens)
     return finish(core.reshape(1), mine, lax.all_gather(theirs, "c", axis=0))
 
 

time: 70 us -> 66.5 us (0.950)
  blocking collectives: 48.3 us -> 42.7 us
  starting transfers between devices: 8.79 us -> 11 us
    all_to_all x1, blocking collectives: 24.2 us -> 18.6 us  [base_term(): lax.all_to_all(parts.reshape(GROUPS, TOKENS // GROUPS, -1), TENSOR, 0, 0,...]
    ppermute x0 -> x1, starting transfers between devices: none -> 5.21 us  [per_device(): near_tokens = lax.ppermute(tokens, ('xl', 'c', 'xh'), pairs)]
    ppermute x1, starting transfers between devices: 8.79 us -> 5.75 us  [per_device(): other = lax.ppermute(blocks, 'c', [(0, 1), (1, 0)])]
    all_gather x1, blocking collectives: 2.3 us -> 4.47 us  [per_device(): return finish(core.reshape(1), mine, lax.all_gather(theirs, 'c', axis=0))]
    all_to_all x1, blocking collectives: 21.8 us -> 19.7 us  [exchange_weights(): weights = lax.all_to_all(weights, 'y', 0, 0, tiled=True)]
    pallas_call x2 -> x3, Pallas kernels: 8.49 us -> 8.35 us  [the longest x1 3.48 us: decode(): pl.pallas_call(decode_kernel, in_specs=[pl.BlockSpec(memory_space=pltpu.S...]
  transfers between devices with their start and end apart: 1 -> 2, of which waited for: 1 -> 1; matrix products, arithmetic and copies ran while one was open for 0% -> 1% of each run, Pallas kernels for 0% -> 8%
where the time goes in v4:
time: 66.5 us; the launch traced here: 66.2 us
  blocking collectives  42.7 us (64%)
  starting transfers between devices  11 us (17%)
  Pallas kernels  9.37 us (14%)
  waiting for transfers between devices  2.63 us (4%)
    all_to_all x1, blocking collectives, exchange_weights(): weights = lax.all_to_all(weights, 'y', 0, 0, tiled=True)  19.7 us
    all_to_all x1, blocking collectives, base_term(): lax.all_to_all(parts.reshape(GROUPS, TOKENS // GROUPS, -1), TENSOR, 0, 0,...  18.6 us
    ppermute x1, starting transfers between devices, per_device(): other = lax.ppermute(blocks, 'c', [(0, 1), (1, 0)])  5.75 us
    ppermute x1, starting transfers between devices, per_device(): near_tokens = lax.ppermute(tokens, ('xl', 'c', 'xh'), pairs)  5.21 us
    all_gather x1, blocking collectives, per_device(): return finish(core.reshape(1), mine, lax.all_gather(theirs, 'c', axis=0))  4.47 us
    pallas_call x1, Pallas kernels, decode(): pl.pallas_call(decode_kernel, in_specs=[pl.BlockSpec(memory_space=pltpu.S...  3.48 us
    pallas_call x1, Pallas kernels, project_near(): pl.pallas_call(project_near_kernel, in_specs=[place, place, pl.BlockSpec(...  3.18 us
    ppermute x1, waiting for transfers between devices, per_device(): other = lax.ppermute(blocks, 'c', [(0, 1), (1, 0)])  2.63 us
  transfers between devices with their start and end apart: 2, of which 1 were waited for; matrix products, arithmetic and copies ran while one was open for 1% of the time, Pallas kernels for 8%

profile of v4, /device:TPU:1, one launch (start us, length us, event | category | flops | bytes accessed | tf_op | source)
XLA Modules:
  0.0 66.2 jit_solution(2317456346168142460)
XLA Ops:
  0.0 5.2 %collective-permute-start.1 = (bf16[1344,1024]{1,0:T(8,128)(2,1)}, bf16[1344,1024]{1,0:T(8,128)(2,1)}, u32[]{:S(2)}, u32[]{:S(2)}) collective-permute-start(bf16[1344,1024]{1,0:T(8,128)(2,1)} %param.13), channel_id=1, source_target_pairs={{8,265},{9,264},{264,9},{265,8},{10,267},{11,266},{266,11},{267,10... | collective-permute-start | bytes 8257544 | tf_op jit(solution)/shard_map/ppermute | solution.py:347
  5.2 3.5 %decode.1 = bf16[5,64,2048]{2,1,0:T(8,128)(2,1)S(1)} custom-call(s32[1]{0:T(128)} %bitcast.3.own, s32[32,8192]{1,0:T(8,128)} %gate_ids.1, s32[32,8192]{1,0:T(8,128)} %up_ids.1, s32[32,128]{1,0:T(8,128)} %gate_powers.1, s32[32,128]{1,0:T(8,128)} %up_powers.1, bf16[32,128]{1,0:T(8,128)(2,1)} %gate_b.1, bf16[32,128]{1,0:T(8,128)(2,1)} %up_b.1, ...), custom_call_target="tpu_custom_call" | custom-call | flops 16777216 | bytes 3145728 | tf_op jit(solution)/shard_map/decode/pallas_call | solution.py:102
  8.7 5.8 %collective-permute-start = (bf16[5,64,2048]{2,1,0:T(8,128)(2,1)S(1)}, bf16[5,64,2048]{2,1,0:T(8,128)(2,1)S(1)}, u32[]{:S(2)}, u32[]{:S(2)}) collective-permute-start(bf16[5,64,2048]{2,1,0:T(8,128)(2,1)S(1)} %decode.1), channel_id=1, source_target_pairs={{0,8},{8,0},{1,9},{9,1},{2,10},{10,2},{3,11},{11,3},{4,12},{12,4},... | collective-permute-start | bytes 3932168 | tf_op jit(solution)/shard_map/ppermute | solution.py:350
  14.5 2.6 %collective-permute-done = bf16[5,64,2048]{2,1,0:T(8,128)(2,1)S(1)} collective-permute-done((bf16[5,64,2048]{2,1,0:T(8,128)(2,1)S(1)}, bf16[5,64,2048]{2,1,0:T(8,128)(2,1)S(1)}, u32[]{:S(2)}, u32[]{:S(2)}) %collective-permute-start) | collective-permute-done | bytes 1310752 | tf_op jit(solution)/shard_map/ppermute | solution.py:350
  17.1 21.9 %conditional.2 = (f32[1344,512]{1,0:T(8,128)S(1)}, bf16[512,1024]{1,0:T(8,128)(2,1)S(1)}, bf16[8,144,128]{2,1,0:T(8,128)(2,1)S(1)}) conditional(s32[]{:T(128)} %convert_element_type.4, (bf16[5,64,2048]{2,1,0:T(8,128)(2,1)S(1)}, bf16[5,64,2048]{2,1,0:T(8,128)(2,1)S(1)}, bf16[1344,1024]{1,0:T(8,128)(2,1)}) %tuple.23, (bf16[1344,1024]{1,0:T(8,128)(2,1)}, ...), branch_computations={%region_0.0_spmd, %region_1.0_spmd} | conditional | flops 1413480448 | bytes 32276534 | solution.py:351
  17.1 0.1 slice.4
  17.2 0.1 slice.5
  17.3 0.2 pad_maximum_fusion
  17.5 0.0 copy-start
  17.5 19.7 %all_to_all.16.weights = bf16[4,128,2048]{2,1,0:T(8,128)(2,1)S(1)} all-to-all(bf16[4,128,2048]{2,1,0:T(8,128)(2,1)S(1)} %pad_maximum_fusion), channel_id=1, replica_groups=mesh['xl'=2,'z'=16,'c'=2,'y'=4,'xh'=2] {'y'}, dimensions={0} | all-to-all | bytes 4194304 | tf_op jit(solution)/shard_map/cond/branch_0_fun/all_to_all | solution.py:322
  37.2 0.0 copy-done
  37.2 1.7 %project_own.1 = (f32[1344,512]{1,0:T(8,128)S(1)}, bf16[512,1024]{1,0:T(8,128)(2,1)S(1)}) custom-call(bf16[4,128,2048]{2,1,0:T(8,128)(2,1)S(1)} %all_to_all.16.weights, bf16[1344,1024]{1,0:T(8,128)(2,1)S(1)} %copy-done), custom_call_target="tpu_custom_call" | custom-call | flops 1409286144 | bytes 8388608 | tf_op jit(solution)/shard_map/cond/branch_0_fun/project_own/pallas_call | solution.py:136
  39.0 0.0 collective-permute-done.1
  39.0 21.9 %conditional.3 = ((f32[168,512]{1,0:T(8,128)S(1)}, f32[168,512]{1,0:T(8,128)S(1)})) conditional(s32[]{:T(128)} %convert_element_type.4, (f32[1344,512]{1,0:T(8,128)S(1)}, bf16[512,1024]{1,0:T(8,128)(2,1)S(1)}, bf16[1344,1024]{1,0:T(8,128)(2,1)}) %tuple.25, bf16[8,144,128]{2,1,0:T(8,128)(2,1)S(1)} %get-tuple-element.43), branch_computations={%region_2.0_spmd, %region_3.0_spmd} | conditional | flops 1411383296 | bytes 14286856 | solution.py:352
  39.0 3.2 %project_near.1 = bf16[1344,512]{1,0:T(8,128)(2,1)S(1)} custom-call(f32[1344,512]{1,0:T(8,128)S(1)} %get-tuple-element.33.total, bf16[512,1024]{1,0:T(8,128)(2,1)S(1)} %get-tuple-element.34.weights, bf16[1344,1024]{1,0:T(8,128)(2,1)} %get-tuple-element.35.tokens), custom_call_target="tpu_custom_call" | custom-call | flops 1409286144 | bytes 8388608 | tf_op jit(solution)/shard_map/cond/branch_0_fun/project_near/pallas_call | solution.py:167
  42.2 18.6 %all_to_all.18.parts = bf16[8,168,512]{2,1,0:T(8,128)(2,1)S(1)} all-to-all(bf16[8,168,512]{2,1,0:T(8,128)(2,1)S(1)} %bitcast.5), channel_id=1, replica_groups=mesh['xl'=2,'z'=16,'c'=2,'y'=4,'xh'=2] {'y','xh'}, dimensions={0} | all-to-all | bytes 2752512 | tf_op jit(solution)/shard_map/cond/branch_0_fun/all_to_all | solution.py:334
  60.7 0.2 add_up.1
  60.9 4.5 %all-gather = f32[336,512]{1,0:T(8,128)S(1)} all-gather(f32[168,512]{1,0:T(8,128)S(1)} %get-tuple-element.45), channel_id=2, replica_groups=mesh['xl'=2,'z'=16,'c'=2,'y'=4,'xh'=2] {'c'}, dimensions={0}, use_global_device_ids=true | all-gather | bytes 1032192 | tf_op jit(solution)/shard_map/all_gather | solution.py:353
  65.4 0.9 %finish.1 = bf16[168,256]{1,0:T(8,128)(2,1)} custom-call(s32[1]{0:T(128)} %bitcast.2.core, f32[168,512]{1,0:T(8,128)S(1)} %get-tuple-element.44.mine, f32[2,168,512]{2,1,0:T(8,128)S(1)} %bitcast.6), custom_call_target="tpu_custom_call" | custom-call | flops 1048576 | bytes 1572864 | tf_op jit(solution)/shard_map/finish/pallas_call | solution.py:309
  (1 shorter events, 0.0 us)
Async XLA Ops:
  0.0 39.0 %collective-permute-start.1 = (bf16[1344,1024]{1,0:T(8,128)(2,1)}, bf16[1344,1024]{1,0:T(8,128)(2,1)}, u32[]{:S(2)}, u32[]{:S(2)}) collective-permute-start(bf16[1344,1024]{1,0:T(8,128)(2,1)} %param.13), channel_id=1, source_target_pairs={{8,265},{9,264},{264,9},{265,8},{10,267},{11,266},{266,11},{267,10... | collective-permute-start | bytes 8257544 | tf_op jit(solution)/shard_map/ppermute | solution.py:347
  8.7 8.4 %collective-permute-start = (bf16[5,64,2048]{2,1,0:T(8,128)(2,1)S(1)}, bf16[5,64,2048]{2,1,0:T(8,128)(2,1)S(1)}, u32[]{:S(2)}, u32[]{:S(2)}) collective-permute-start(bf16[5,64,2048]{2,1,0:T(8,128)(2,1)S(1)} %decode.1), channel_id=1, source_target_pairs={{0,8},{8,0},{1,9},{9,1},{2,10},{10,2},{3,11},{11,3},{4,12},{12,4},... | collective-permute-start | bytes 3932168 | tf_op jit(solution)/shard_map/ppermute | solution.py:350
  17.5 19.7 %copy-start = (bf16[1344,1024]{1,0:T(8,128)(2,1)S(1)}, bf16[1344,1024]{1,0:T(8,128)(2,1)}, u32[]{:S(2)}) copy-start(bf16[1344,1024]{1,0:T(8,128)(2,1)} %get-tuple-element.27.tokens) | copy-start | bytes 8257540 | tf_op jit(solution)/shard_map/cond

commit v5 on v4

--- a/solution.py
+++ b/solution.py
@@ -16,6 +16,7 @@
 LANES = 128
 PAIRS = 4
 PIECES = 2
+HELD = 2 * 4 * 32
 SIDE = 144
 
 NF4_LEVELS = (
@@ -56,8 +57,9 @@
     for p, (powers, factor, a) in enumerate(((gate_powers, gate_b, gate_a), (up_powers, up_b, up_a))):
         extra.append(pltpu.make_async_copy(powers, small.at[p], near.at[p]))
         extra.append(pltpu.make_async_copy(a, thin.at[p], near.at[2 + p]))
-        place = out.at[PAIRS, pl.ds(p * ROWS, ROWS), pl.ds(0, RANK)]
-        stores.append(pltpu.make_async_copy(factor, place, sent.at[PAIRS + 1 + p]))
+        for h in range(2):
+            place = out.at[pl.ds(HELD, 16), pl.ds((2 * p + h) * RANK, RANK)]
+            stores.append(pltpu.make_async_copy(factor.at[pl.ds(h * 16, 16)], place, sent.at[PAIRS + 1 + 2 * p + h]))
     loads, groups = [], []
     for k in range(GROUPS):
         group = k // 2 * 2 + (own[0] + k % 2) % 2
@@ -71,33 +73,31 @@
     for copy in extra:
         copy.wait()
     rows = jnp.concatenate([thin[0].astype(jnp.float32), thin[1].astype(jnp.float32), jnp.zeros((12, WIDTH), jnp.float32)], axis=0)
-    blocks[PAIRS, pl.ds(0, 16), pl.ds(0, WIDTH)] = rows.astype(jnp.bfloat16)
-    stores.append(
-        pltpu.make_async_copy(
-            blocks.at[PAIRS, pl.ds(0, 16), pl.ds(0, WIDTH)], out.at[PAIRS, pl.ds(0, 16), pl.ds(WIDTH, WIDTH)], sent.at[PAIRS]
-        )
-    )
+    blocks[pl.ds(HELD, 16), pl.ds(WIDTH, WIDTH)] = rows.astype(jnp.bfloat16)
+    last = (pl.ds(HELD, 16), pl.ds(WIDTH, WIDTH))
+    stores.append(pltpu.make_async_copy(blocks.at[last], out.at[last], sent.at[PAIRS]))
     stores[-1].start()
     half = lax.broadcasted_iota(jnp.int32, (ROWS, LANES), 1) // BLOCK
     scales = [(jnp.int32(1) << (small[p] + 8)).astype(jnp.float32) * 2.0**-8 for p in range(2)]
     for k in range(GROUPS):
         for p in range(2):
             loads[k][p].wait()
-            rows = pl.ds(p * ROWS, ROWS)
+            rows = pl.ds(k // 2 * 2 * ROWS + p * ROWS, ROWS)
             for chunk in range(WIDTH // LANES):
                 level = pick(ids[p, k, :, pl.ds(chunk * LANES, LANES)].astype(jnp.int16), 0, len(LEVELS))
                 scale = lookup(scales[p], half + (groups[k] * (WIDTH // BLOCK) + chunk * (LANES // BLOCK)))
                 columns = pl.ds(k % 2 * WIDTH + chunk * LANES, LANES)
-                blocks[k // 2, rows, columns] = level * scale.astype(jnp.bfloat16)
+                blocks[rows, columns] = level * scale.astype(jnp.bfloat16)
         if k % 2:
-            stores.append(pltpu.make_async_copy(blocks.at[k // 2], out.at[k // 2], sent.at[k // 2]))
+            rows = pl.ds(k // 2 * 2 * ROWS, 2 * ROWS)
+            stores.append(pltpu.make_async_copy(blocks.at[rows], out.at[rows], sent.at[k // 2]))
             stores[-1].start()
     for store in stores:
         store.wait()
 
 
 def decode(*args):
-    shape = (PAIRS + 1, 2 * ROWS, 2 * WIDTH)
+    shape = (HELD + 16, 2 * WIDTH)
     hbm = pl.BlockSpec(memory_space=pltpu.HBM)
     return pl.pallas_call(
         decode_kernel,
@@ -111,7 +111,7 @@
             pltpu.VMEM(shape, jnp.bfloat16),
             pltpu.SemaphoreType.DMA((2, GROUPS)),
             pltpu.SemaphoreType.DMA((4,)),
-            pltpu.SemaphoreType.DMA((PAIRS + 3,)),
+            pltpu.SemaphoreType.DMA((PAIRS + 5,)),
         ],
         compiler_params=pltpu.CompilerParams(vmem_limit_bytes=62 * 2**20),
         cost_estimate=pl.CostEstimate(flops=2**24, bytes_accessed=3 * 2**20, transcendentals=0),
@@ -198,26 +198,35 @@
     )(parts)
 
 
-def shrink_kernel(first, second, tokens, out):
-    a = [block[0, pl.ds(0, 16), pl.ds(WIDTH, WIDTH)].astype(jnp.float32)[0:4] for block in (first, second)]
+def shrink_kernel(first, second, tokens, out, *rest):
+    a = [block[:, pl.ds(WIDTH, WIDTH)].astype(jnp.float32)[0:4] for block in (first, second)]
     a = jnp.concatenate(a, axis=0).astype(jnp.bfloat16)
     count = TOKENS // GROUPS
-    for k in range(GROUPS):
-        out[k, pl.ds(0, 2 * ROWS), :] = first[0, :, pl.ds(0, RANK)]
-        out[k, pl.ds(2 * ROWS, 2 * ROWS), :] = second[0, :, pl.ds(0, RANK)]
+    step = pl.program_id(0) * tokens.shape[0]
+    for k in range(tokens.shape[0]):
+        for c, block in enumerate((first, second)):
+            for h in range(4):
+                out[step + k, pl.ds(c * 2 * ROWS + h * 16, 16), :] = block[:, pl.ds(h * RANK, RANK)]
         product = lax.dot_general(a, tokens[k], (((1,), (1,)), ((), ())), preferred_element_type=jnp.float32)
-        rest = jnp.concatenate([product[:, LANES:], jnp.zeros((8, 2 * LANES - count), jnp.float32)], axis=1)
-        out[k, pl.ds(4 * ROWS, 16), :] = jnp.concatenate([product[:, :LANES], rest], axis=0).astype(jnp.bfloat16)
-
-
-def shrink(first, second, tokens):
-    side = pl.BlockSpec((1, 2 * ROWS, 2 * WIDTH), lambda i: (PAIRS, 0, 0))
+        high = jnp.concatenate([product[:, LANES:], jnp.zeros((8, 2 * LANES - count), jnp.float32)], axis=1)
+        both = jnp.concatenate([product[:, :LANES], high], axis=0)
+        out[step + k, pl.ds(4 * ROWS, 16), :] = both.astype(jnp.bfloat16)
+
+
+def shrink(first, second, tokens, steps=2):
+    side = pl.BlockSpec((16, 2 * WIDTH), lambda i: (HELD // 16, 0))
+    columns = 4 * PAIRS * ROWS
+    room = pl.BlockSpec(memory_space=pl.ANY)
     return pl.pallas_call(
         shrink_kernel,
-        grid=(1,),
-        in_specs=[side, side, pl.BlockSpec((GROUPS, TOKENS // GROUPS, WIDTH), lambda i: (0, 0, 0))],
-        out_specs=pl.BlockSpec((GROUPS, SIDE, LANES), lambda i: (0, 0, 0)),
-        out_shape=jax.ShapeDtypeStruct((GROUPS, SIDE, LANES), jnp.bfloat16),
+        grid=(steps,),
+        in_specs=[side, side, pl.BlockSpec((GROUPS // steps, TOKENS // GROUPS, WIDTH), lambda i: (i, 0, 0))],
+        out_specs=[pl.BlockSpec((GROUPS, SIDE, LANES), lambda i: (0, 0, 0)), room, room],
+        out_shape=[
+            jax.ShapeDtypeStruct((GROUPS, SIDE, LANES), jnp.bfloat16),
+            jax.ShapeDtypeStruct((TOKENS, columns), jnp.float32),
+            jax.ShapeDtypeStruct((columns, WIDTH), jnp.bfloat16),
+        ],
         compiler_params=pltpu.CompilerParams(vmem_limit_bytes=40 * 2**20),
         cost_estimate=pl.CostEstimate(flops=2**24, bytes_accessed=3 * 2**20, transcendentals=0),
         name="shrink",
@@ -318,15 +327,14 @@
 
 
 def exchange_weights(blocks, other, tokens):
-    weights = jnp.concatenate([other[:PAIRS], blocks[:PAIRS]], axis=1)
+    weights = jnp.concatenate([part[:HELD].reshape(PAIRS, 2 * ROWS, 2 * WIDTH) for part in (other, blocks)], axis=1)
     weights = lax.all_to_all(weights, "y", 0, 0, tiled=True)
     return *project_own(weights, tokens), jnp.zeros((GROUPS, SIDE, LANES), jnp.bfloat16)
 
 
 def exchange_shrunk(blocks, other, tokens):
-    side = lax.all_to_all(shrink(blocks, other, tokens), TENSOR, 0, 0, tiled=True)
-    columns = 4 * PAIRS * ROWS
-    return jnp.zeros((TOKENS, columns), jnp.float32), jnp.zeros((columns, WIDTH), jnp.bfloat16), side
+    side, total, weights = shrink(blocks, other, tokens)
+    return total, weights, lax.all_to_all(side, TENSOR, 0, 0, tiled=True)
 
 
 def base_term(total, weights, side, near_tokens):

time: 66.5 us -> 65.5 us (0.985)
  blocking collectives: 42.7 us -> 41.9 us
    all_gather x1, blocking collectives: 4.47 us -> 3.48 us  [per_device(): return finish(core.reshape(1), mine, lax.all_gather(theirs, 'c', axis=0))]
where the time goes in v5:
time: 65.5 us; the launch traced here: 65.2 us
  blocking collectives  41.9 us (64%)
  starting transfers between devices  11 us (17%)
  Pallas kernels  9.4 us (14%)
  waiting for transfers between devices  2.35 us (4%)
    all_to_all x1, blocking collectives, exchange_weights(): weights = lax.all_to_all(weights, 'y', 0, 0, tiled=True)  19.7 us
    all_to_all x1, blocking collectives, base_term(): lax.all_to_all(parts.reshape(GROUPS, TOKENS // GROUPS, -1), TENSOR, 0, 0,...  18.7 us
    ppermute x1, starting transfers between devices, per_device(): other = lax.ppermute(blocks, 'c', [(0, 1), (1, 0)])  5.75 us
    ppermute x1, starting transfers between devices, per_device(): near_tokens = lax.ppermute(tokens, ('xl', 'c', 'xh'), pairs)  5.21 us
    pallas_call x1, Pallas kernels, decode(): pl.pallas_call(decode_kernel, in_specs=[pl.BlockSpec(memory_space=pltpu.S...  3.51 us
    all_gather x1, blocking collectives, per_device(): return finish(core.reshape(1), mine, lax.all_gather(theirs, 'c', axis=0))  3.48 us
    pallas_call x1, Pallas kernels, project_near(): pl.pallas_call(project_near_kernel, in_specs=[place, place, pl.BlockSpec(...  3.18 us
    ppermute x1, waiting for transfers between devices, per_device(): other = lax.ppermute(blocks, 'c', [(0, 1), (1, 0)])  2.35 us
  transfers between devices with their start and end apart: 2, of which 1 were waited for; matrix products, arithmetic and copies ran while one was open for 1% of the time, Pallas kernels for 8%

profile of v5, /device:TPU:1, one launch (start us, length us, event | category | flops | bytes accessed | tf_op | source)
XLA Modules:
  0.0 65.2 jit_solution(6043927079736749943)
XLA Ops:
  0.0 5.2 %collective-permute-start.1 = (bf16[1344,1024]{1,0:T(8,128)(2,1)}, bf16[1344,1024]{1,0:T(8,128)(2,1)}, u32[]{:S(2)}, u32[]{:S(2)}) collective-permute-start(bf16[1344,1024]{1,0:T(8,128)(2,1)} %param.13), channel_id=1, source_target_pairs={{8,265},{9,264},{264,9},{265,8},{10,267},{11,266},{266,11},{267,10... | collective-permute-start | bytes 8257544 | tf_op jit(solution)/shard_map/ppermute | solution.py:355
  5.2 3.5 %decode.1 = bf16[272,2048]{1,0:T(8,128)(2,1)S(1)} custom-call(s32[1]{0:T(128)} %bitcast.5.own, s32[32,8192]{1,0:T(8,128)} %gate_ids.1, s32[32,8192]{1,0:T(8,128)} %up_ids.1, s32[32,128]{1,0:T(8,128)} %gate_powers.1, s32[32,128]{1,0:T(8,128)} %up_powers.1, bf16[32,128]{1,0:T(8,128)(2,1)} %gate_b.1, bf16[32,128]{1,0:T(8,128)(2,1)} %up_b.1, ...), custom_call_target="tpu_custom_call" | custom-call | flops 16777216 | bytes 3145728 | tf_op jit(solution)/shard_map/decode/pallas_call | solution.py:102
  8.7 5.7 %collective-permute-start = (bf16[272,2048]{1,0:T(8,128)(2,1)S(1)}, bf16[272,2048]{1,0:T(8,128)(2,1)S(1)}, u32[]{:S(2)}, u32[]{:S(2)}) collective-permute-start(bf16[272,2048]{1,0:T(8,128)(2,1)S(1)} %decode.1), channel_id=1, source_target_pairs={{0,8},{8,0},{1,9},{9,1},{2,10},{10,2},{3,11},{11,3},{4,12},{12,4},... | collective-permute-start | bytes 3342344 | tf_op jit(solution)/shard_map/ppermute | solution.py:358
  14.5 2.4 %collective-permute-done = bf16[272,2048]{1,0:T(8,128)(2,1)S(1)} collective-permute-done((bf16[272,2048]{1,0:T(8,128)(2,1)S(1)}, bf16[272,2048]{1,0:T(8,128)(2,1)S(1)}, u32[]{:S(2)}, u32[]{:S(2)}) %collective-permute-start) | collective-permute-done | bytes 1114144 | tf_op jit(solution)/shard_map/ppermute | solution.py:358
  16.9 21.9 %conditional.2 = (f32[1344,512]{1,0:T(8,128)S(1)}, bf16[512,1024]{1,0:T(8,128)(2,1)S(1)}, bf16[8,144,128]{2,1,0:T(8,128)(2,1)S(1)}) conditional(s32[]{:T(128)} %convert_element_type.4, (bf16[272,2048]{1,0:T(8,128)(2,1)S(1)}, bf16[272,2048]{1,0:T(8,128)(2,1)S(1)}, bf16[1344,1024]{1,0:T(8,128)(2,1)}) %tuple.23, (bf16[1344,1024]{1,0:T(8,128)(2,1)}, ...), branch_computations={%region_0.0_spmd, %region_1.0_spmd} | conditional | flops 1413480448 | bytes 32276534 | solution.py:359
  16.9 0.1 slice.4
  16.9 0.1 slice.5
  17.0 0.2 pad_maximum_fusion
  17.3 0.0 copy-start
  17.3 19.7 %all_to_all.16.weights = bf16[4,128,2048]{2,1,0:T(8,128)(2,1)S(1)} all-to-all(bf16[4,128,2048]{2,1,0:T(8,128)(2,1)S(1)} %pad_maximum_fusion), channel_id=1, replica_groups=mesh['xl'=2,'z'=16,'c'=2,'y'=4,'xh'=2] {'y'}, dimensions={0} | all-to-all | bytes 4194304 | tf_op jit(solution)/shard_map/cond/branch_0_fun/all_to_all | solution.py:331
  37.0 0.0 copy-done
  37.0 1.7 %project_own.1 = (f32[1344,512]{1,0:T(8,128)S(1)}, bf16[512,1024]{1,0:T(8,128)(2,1)S(1)}) custom-call(bf16[4,128,2048]{2,1,0:T(8,128)(2,1)S(1)} %all_to_all.16.weights, bf16[1344,1024]{1,0:T(8,128)(2,1)S(1)} %copy-done), custom_call_target="tpu_custom_call" | custom-call | flops 1409286144 | bytes 8388608 | tf_op jit(solution)/shard_map/cond/branch_0_fun/project_own/pallas_call | solution.py:136
  38.7 0.0 collective-permute-done.1
  38.7 22.1 %conditional.3 = ((f32[168,512]{1,0:T(8,128)S(1)}, f32[168,512]{1,0:T(8,128)S(1)})) conditional(s32[]{:T(128)} %convert_element_type.4, (f32[1344,512]{1,0:T(8,128)S(1)}, bf16[512,1024]{1,0:T(8,128)(2,1)S(1)}, bf16[1344,1024]{1,0:T(8,128)(2,1)}) %tuple.25, bf16[8,144,128]{2,1,0:T(8,128)(2,1)S(1)} %get-tuple-element.46), branch_computations={%region_2.0_spmd, %region_3.0_spmd} | conditional | flops 1411383296 | bytes 14286856 | solution.py:360
  38.7 3.2 %project_near.1 = bf16[1344,512]{1,0:T(8,128)(2,1)S(1)} custom-call(f32[1344,512]{1,0:T(8,128)S(1)} %get-tuple-element.36.total, bf16[512,1024]{1,0:T(8,128)(2,1)S(1)} %get-tuple-element.37.weights, bf16[1344,1024]{1,0:T(8,128)(2,1)} %get-tuple-element.38.tokens), custom_call_target="tpu_custom_call" | custom-call | flops 1409286144 | bytes 8388608 | tf_op jit(solution)/shard_map/cond/branch_0_fun/project_near/pallas_call | solution.py:167
  41.9 18.7 %all_to_all.18.parts = bf16[8,168,512]{2,1,0:T(8,128)(2,1)S(1)} all-to-all(bf16[8,168,512]{2,1,0:T(8,128)(2,1)S(1)} %bitcast.7), channel_id=1, replica_groups=mesh['xl'=2,'z'=16,'c'=2,'y'=4,'xh'=2] {'y','xh'}, dimensions={0} | all-to-all | bytes 2752512 | tf_op jit(solution)/shard_map/cond/branch_0_fun/all_to_all | solution.py:342
  60.7 0.2 add_up.1
  60.8 3.5 %all-gather = f32[336,512]{1,0:T(8,128)S(1)} all-gather(f32[168,512]{1,0:T(8,128)S(1)} %get-tuple-element.48), channel_id=2, replica_groups=mesh['xl'=2,'z'=16,'c'=2,'y'=4,'xh'=2] {'c'}, dimensions={0}, use_global_device_ids=true | all-gather | bytes 1032192 | tf_op jit(solution)/shard_map/all_gather | solution.py:361
  64.3 0.9 %finish.1 = bf16[168,256]{1,0:T(8,128)(2,1)} custom-call(s32[1]{0:T(128)} %bitcast.4.core, f32[168,512]{1,0:T(8,128)S(1)} %get-tuple-element.47.mine, f32[2,168,512]{2,1,0:T(8,128)S(1)} %bitcast.8), custom_call_target="tpu_custom_call" | custom-call | flops 1048576 | bytes 1572864 | tf_op jit(solution)/shard_map/finish/pallas_call | solution.py:318
  (1 shorter events, 0.0 us)
Async XLA Ops:
  0.0 38.7 %collective-permute-start.1 = (bf16[1344,1024]{1,0:T(8,128)(2,1)}, bf16[1344,1024]{1,0:T(8,128)(2,1)}, u32[]{:S(2)}, u32[]{:S(2)}) collective-permute-start(bf16[1344,1024]{1,0:T(8,128)(2,1)} %param.13), channel_id=1, source_target_pairs={{8,265},{9,264},{264,9},{265,8},{10,267},{11,266},{266,11},{267,10... | collective-permute-start | bytes 8257544 | tf_op jit(solution)/shard_map/ppermute | solution.py:355
  8.7 8.1 %collective-permute-start = (bf16[272,2048]{1,0:T(8,128)(2,1)S(1)}, bf16[272,2048]{1,0:T(8,128)(2,1)S(1)}, u32[]{:S(2)}, u32[]{:S(2)}) collective-permute-start(bf16[272,2048]{1,0:T(8,128)(2,1)S(1)} %decode.1), channel_id=1, source_target_pairs={{0,8},{8,0},{1,9},{9,1},{2,10},{10,2},{3,11},{11,3},{4,12},{12,4},... | collective-permute-start | bytes 3342344 | tf_op jit(solution)/shard_map/ppermute | solution.py:358
  17.3 19.7 %copy-start = (bf16[1344,1024]{1,0:T(8,128)(2,1)S(1)}, bf16[1344,1024]{1,0:T(8,128)(2,1)}, u32[]{:S(2)}) copy-start(bf16[1344,1024]{1,0:T(8,128)(2,1)} %get-tuple-element.27.tokens) | copy-start | bytes 8257540 | tf_op jit(solution)/shard_map/cond

commit v6 on v5

--- a/solution.py
+++ b/solution.py
@@ -184,14 +184,14 @@
             total = total + parts[2 * y + x].astype(jnp.float32)
         for q in range(4):
             to = theirs if q < 2 else mine
-            to[:, pl.ds((q % 2 * 2 + x) * part, part)] = total[:, q * part : (q + 1) * part]
+            to[:, pl.ds((q % 2 * 2 + x) * part, part)] = total[:, q * part : (q + 1) * part].astype(to.dtype)
 
 
 def add_up(parts):
-    shape = jax.ShapeDtypeStruct((parts.shape[1], parts.shape[2]), jnp.float32)
+    shape = (parts.shape[1], parts.shape[2])
     return pl.pallas_call(
         add_up_kernel,
-        out_shape=[shape, shape],
+        out_shape=[jax.ShapeDtypeStruct(shape, jnp.float32), jax.ShapeDtypeStruct(shape, jnp.bfloat16)],
         compiler_params=pltpu.CompilerParams(vmem_limit_bytes=32 * 2**20),
         cost_estimate=pl.CostEstimate(flops=2**21, bytes_accessed=3 * 2**20, transcendentals=0),
         name="add_up",
@@ -253,8 +253,10 @@
 def spread_kernel(side, out):
     rank = lax.broadcasted_iota(jnp.int32, (RANK, 2 * RANK), 0)
     place = lax.broadcasted_iota(jnp.int32, (RANK, 2 * RANK), 1)
+    slot = place // 4
+    owner = slot // 2 % 2 * 32 + slot // 4 * 2 + slot % 2
     for q in range(4):
-        hit = (place % 4 // 2 == q % 2) & (place // 4 * 2 + place % 2 == rank)
+        hit = (place % 4 // 2 == q % 2) & (owner * 2 + place % 2 == rank)
         factor = jnp.concatenate([side[k, pl.ds(q * ROWS, ROWS), :] for k in (0, 2, 4, 6, 1, 3, 5, 7)], axis=0)
         out[q] = jnp.dot(
             factor, hit.astype(jnp.float32).astype(jnp.bfloat16), preferred_element_type=jnp.float32
@@ -282,17 +284,17 @@
         columns = pl.ds(q % 2 * half, half)
         to[pl.ds(0, LANES), columns] = lax.dot_general(
             low, factors[q], (((1,), (1,)), ((), ())), preferred_element_type=jnp.float32
-        )
+        ).astype(to.dtype)
         to[pl.ds(LANES, count - LANES), columns] = lax.dot_general(
             high, factors[q], (((1,), (1,)), ((), ())), preferred_element_type=jnp.float32
-        )[: count - LANES]
+        )[: count - LANES].astype(to.dtype)
 
 
 def grow(factors, shrunk):
-    shape = jax.ShapeDtypeStruct((TOKENS // GROUPS, 2 * GROUPS * ROWS), jnp.float32)
+    shape = (TOKENS // GROUPS, 2 * GROUPS * ROWS)
     return pl.pallas_call(
         grow_kernel,
-        out_shape=[shape, shape],
+        out_shape=[jax.ShapeDtypeStruct(shape, jnp.float32), jax.ShapeDtypeStruct(shape, jnp.bfloat16)],
         compiler_params=pltpu.CompilerParams(vmem_limit_bytes=32 * 2**20),
         cost_estimate=pl.CostEstimate(flops=2**25, bytes_accessed=2**20, transcendentals=0),
         name="grow",
@@ -302,8 +304,8 @@
 def finish_kernel(core, mine, both, out):
     half = GROUPS * ROWS
     other = both.at[1 - core[0]]
-    gate = mine[:, :half] + other[:, :half]
-    up = mine[:, half:] + other[:, half:]
+    gate = mine[:, :half] + other[:, :half].astype(jnp.float32)
+    up = mine[:, half:] + other[:, half:].astype(jnp.float32)
     result = (gate / (1.0 + jnp.exp(-gate)) * up).astype(jnp.bfloat16)
     place = lax.broadcasted_iota(jnp.int32, (half, half), 0)
     column = lax.broadcasted_iota(jnp.int32, (half, half), 1)
@@ -345,7 +347,7 @@
 
 def adapter_term(total, weights, side, near_tokens):
     copies = copies_of(side, lax.axis_size("xl") * lax.axis_size("z"))
-    shrunk = lax.all_to_all(copies, ("xl", "z"), 0, 0, tiled=True)
+    shrunk = lax.all_to_all(copies, ("z", "xl"), 0, 0, tiled=True)
     return tuple(grow(spread_out(side), shrunk))
 
 

time: 65.5 us -> 64.6 us (0.986)
  blocking collectives: 41.9 us -> 41 us
    all_gather x1, blocking collectives: 3.48 us -> 2.59 us  [per_device(): return finish(core.reshape(1), mine, lax.all_gather(theirs, 'c', axis=0))]
where the time goes in v6:
time: 64.6 us; the launch traced here: 64.3 us
  blocking collectives  41 us (63%)
  starting transfers between devices  11 us (17%)
  Pallas kernels  9.42 us (15%)
  waiting for transfers between devices  2.35 us (4%)
    all_to_all x1, blocking collectives, exchange_weights(): weights = lax.all_to_all(weights, 'y', 0, 0, tiled=True)  19.7 us
    all_to_all x1, blocking collectives, base_term(): lax.all_to_all(parts.reshape(GROUPS, TOKENS // GROUPS, -1), TENSOR, 0, 0,...  18.8 us
    ppermute x1, starting transfers between devices, per_device(): other = lax.ppermute(blocks, 'c', [(0, 1), (1, 0)])  5.75 us
    ppermute x1, starting transfers between devices, per_device(): near_tokens = lax.ppermute(tokens, ('xl', 'c', 'xh'), pairs)  5.21 us
    pallas_call x1, Pallas kernels, decode(): pl.pallas_call(decode_kernel, in_specs=[pl.BlockSpec(memory_space=pltpu.S...  3.51 us
    pallas_call x1, Pallas kernels, project_near(): pl.pallas_call(project_near_kernel, in_specs=[place, place, pl.BlockSpec(...  3.18 us
    all_gather x1, blocking collectives, per_device(): return finish(core.reshape(1), mine, lax.all_gather(theirs, 'c', axis=0))  2.59 us
    ppermute x1, waiting for transfers between devices, per_device(): other = lax.ppermute(blocks, 'c', [(0, 1), (1, 0)])  2.35 us
  transfers between devices with their start and end apart: 2, of which 1 were waited for; matrix products, arithmetic and copies ran while one was open for 1% of the time, Pallas kernels for 8%

profile of v6, /device:TPU:1, one launch (start us, length us, event | category | flops | bytes accessed | tf_op | source)
XLA Modules:
  0.0 64.3 jit_solution(16258757628441935406)
XLA Ops:
  0.0 5.2 %collective-permute-start.1 = (bf16[1344,1024]{1,0:T(8,128)(2,1)}, bf16[1344,1024]{1,0:T(8,128)(2,1)}, u32[]{:S(2)}, u32[]{:S(2)}) collective-permute-start(bf16[1344,1024]{1,0:T(8,128)(2,1)} %param.13), channel_id=1, source_target_pairs={{8,265},{9,264},{264,9},{265,8},{10,267},{11,266},{266,11},{267,10... | collective-permute-start | bytes 8257544 | tf_op jit(solution)/shard_map/ppermute | solution.py:357
  5.2 3.5 %decode.1 = bf16[272,2048]{1,0:T(8,128)(2,1)S(1)} custom-call(s32[1]{0:T(128)} %bitcast.5.own, s32[32,8192]{1,0:T(8,128)} %gate_ids.1, s32[32,8192]{1,0:T(8,128)} %up_ids.1, s32[32,128]{1,0:T(8,128)} %gate_powers.1, s32[32,128]{1,0:T(8,128)} %up_powers.1, bf16[32,128]{1,0:T(8,128)(2,1)} %gate_b.1, bf16[32,128]{1,0:T(8,128)(2,1)} %up_b.1, ...), custom_call_target="tpu_custom_call" | custom-call | flops 16777216 | bytes 3145728 | tf_op jit(solution)/shard_map/decode/pallas_call | solution.py:102
  8.7 5.7 %collective-permute-start = (bf16[272,2048]{1,0:T(8,128)(2,1)S(1)}, bf16[272,2048]{1,0:T(8,128)(2,1)S(1)}, u32[]{:S(2)}, u32[]{:S(2)}) collective-permute-start(bf16[272,2048]{1,0:T(8,128)(2,1)S(1)} %decode.1), channel_id=1, source_target_pairs={{0,8},{8,0},{1,9},{9,1},{2,10},{10,2},{3,11},{11,3},{4,12},{12,4},... | collective-permute-start | bytes 3342344 | tf_op jit(solution)/shard_map/ppermute | solution.py:360
  14.5 2.4 %collective-permute-done = bf16[272,2048]{1,0:T(8,128)(2,1)S(1)} collective-permute-done((bf16[272,2048]{1,0:T(8,128)(2,1)S(1)}, bf16[272,2048]{1,0:T(8,128)(2,1)S(1)}, u32[]{:S(2)}, u32[]{:S(2)}) %collective-permute-start) | collective-permute-done | bytes 1114144 | tf_op jit(solution)/shard_map/ppermute | solution.py:360
  16.9 21.9 %conditional.2 = (f32[1344,512]{1,0:T(8,128)S(1)}, bf16[512,1024]{1,0:T(8,128)(2,1)S(1)}, bf16[8,144,128]{2,1,0:T(8,128)(2,1)S(1)}) conditional(s32[]{:T(128)} %convert_element_type.4, (bf16[272,2048]{1,0:T(8,128)(2,1)S(1)}, bf16[272,2048]{1,0:T(8,128)(2,1)S(1)}, bf16[1344,1024]{1,0:T(8,128)(2,1)}) %tuple.23, (bf16[1344,1024]{1,0:T(8,128)(2,1)}, ...), branch_computations={%region_0.0_spmd, %region_1.0_spmd} | conditional | flops 1413480448 | bytes 32276534 | solution.py:361
  16.9 0.1 slice.4
  16.9 0.1 slice.5
  17.0 0.2 pad_maximum_fusion
  17.3 0.0 copy-start
  17.3 19.7 %all_to_all.16.weights = bf16[4,128,2048]{2,1,0:T(8,128)(2,1)S(1)} all-to-all(bf16[4,128,2048]{2,1,0:T(8,128)(2,1)S(1)} %pad_maximum_fusion), channel_id=1, replica_groups=mesh['xl'=2,'z'=16,'c'=2,'y'=4,'xh'=2] {'y'}, dimensions={0} | all-to-all | bytes 4194304 | tf_op jit(solution)/shard_map/cond/branch_0_fun/all_to_all | solution.py:333
  37.0 0.0 copy-done
  37.0 1.7 %project_own.1 = (f32[1344,512]{1,0:T(8,128)S(1)}, bf16[512,1024]{1,0:T(8,128)(2,1)S(1)}) custom-call(bf16[4,128,2048]{2,1,0:T(8,128)(2,1)S(1)} %all_to_all.16.weights, bf16[1344,1024]{1,0:T(8,128)(2,1)S(1)} %copy-done), custom_call_target="tpu_custom_call" | custom-call | flops 1409286144 | bytes 8388608 | tf_op jit(solution)/shard_map/cond/branch_0_fun/project_own/pallas_call | solution.py:136
  38.7 0.0 collective-permute-done.1
  38.7 22.1 %conditional.3 = ((f32[168,512]{1,0:T(8,128)S(1)}, bf16[168,512]{1,0:T(8,128)(2,1)S(1)})) conditional(s32[]{:T(128)} %convert_element_type.4, (f32[1344,512]{1,0:T(8,128)S(1)}, bf16[512,1024]{1,0:T(8,128)(2,1)S(1)}, bf16[1344,1024]{1,0:T(8,128)(2,1)}) %tuple.25, bf16[8,144,128]{2,1,0:T(8,128)(2,1)S(1)} %get-tuple-element.46), branch_computations={%region_2.0_spmd, %region_3.0_spmd} | conditional | flops 1411383296 | bytes 14286856 | solution.py:362
  38.7 3.2 %project_near.1 = bf16[1344,512]{1,0:T(8,128)(2,1)S(1)} custom-call(f32[1344,512]{1,0:T(8,128)S(1)} %get-tuple-element.36.total, bf16[512,1024]{1,0:T(8,128)(2,1)S(1)} %get-tuple-element.37.weights, bf16[1344,1024]{1,0:T(8,128)(2,1)} %get-tuple-element.38.tokens), custom_call_target="tpu_custom_call" | custom-call | flops 1409286144 | bytes 8388608 | tf_op jit(solution)/shard_map/cond/branch_0_fun/project_near/pallas_call | solution.py:167
  41.9 18.8 %all_to_all.18.parts = bf16[8,168,512]{2,1,0:T(8,128)(2,1)S(1)} all-to-all(bf16[8,168,512]{2,1,0:T(8,128)(2,1)S(1)} %bitcast.7), channel_id=1, replica_groups=mesh['xl'=2,'z'=16,'c'=2,'y'=4,'xh'=2] {'y','xh'}, dimensions={0} | all-to-all | bytes 2752512 | tf_op jit(solution)/shard_map/cond/branch_0_fun/all_to_all | solution.py:344
  60.7 0.2 add_up.1
  60.9 2.6 %all-gather = bf16[336,512]{1,0:T(8,128)(2,1)S(1)} all-gather(bf16[168,512]{1,0:T(8,128)(2,1)S(1)} %get-tuple-element.48), channel_id=2, replica_groups=mesh['xl'=2,'z'=16,'c'=2,'y'=4,'xh'=2] {'c'}, dimensions={0}, use_global_device_ids=true | all-gather | bytes 516096 | tf_op jit(solution)/shard_map/all_gather | solution.py:363
  63.5 0.9 %finish.1 = bf16[168,256]{1,0:T(8,128)(2,1)} custom-call(s32[1]{0:T(128)} %bitcast.4.core, f32[168,512]{1,0:T(8,128)S(1)} %get-tuple-element.47.mine, bf16[2,168,512]{2,1,0:T(8,128)(2,1)S(1)} %bitcast.8), custom_call_target="tpu_custom_call" | custom-call | flops 1048576 | bytes 1572864 | tf_op jit(solution)/shard_map/finish/pallas_call | solution.py:320
  (1 shorter events, 0.0 us)
Async XLA Ops:
  0.0 38.7 %collective-permute-start.1 = (bf16[1344,1024]{1,0:T(8,128)(2,1)}, bf16[1344,1024]{1,0:T(8,128)(2,1)}, u32[]{:S(2)}, u32[]{:S(2)}) collective-permute-start(bf16[1344,1024]{1,0:T(8,128)(2,1)} %param.13), channel_id=1, source_target_pairs={{8,265},{9,264},{264,9},{265,8},{10,267},{11,266},{266,11},{267,10... | collective-permute-start | bytes 8257544 | tf_op jit(solution)/shard_map/ppermute | solution.py:357
  8.7 8.1 %collective-permute-start = (bf16[272,2048]{1,0:T(8,128)(2,1)S(1)}, bf16[272,2048]{1,0:T(8,128)(2,1)S(1)}, u32[]{:S(2)}, u32[]{:S(2)}) collective-permute-start(bf16[272,2048]{1,0:T(8,128)(2,1)S(1)} %decode.1), channel_id=1, source_target_pairs={{0,8},{8,0},{1,9},{9,1},{2,10},{10,2},{3,11},{11,3},{4,12},{12,4},... | collective-permute-start | bytes 3342344 | tf_op jit(solution)/shard_map/ppermute | solution.py:360
  17.3 19.7 %copy-start = (bf16[1344,1024]{1,0:T(8,128)(2,1)S(1)}, bf16[1344,1024]{1,0:T(8,128)(2,1)}, u32[]{:S(2)}) copy-start(bf16[1344,1024]{1,0:T(8,128)(2,1)} %get-tuple-element.27.tokens) | copy-start | bytes 8257540 | tf_op jit(solution)/shard_map/cond

commit v7 on v6

--- a/solution.py
+++ b/solution.py
@@ -52,14 +52,14 @@
     return jnp.take_along_axis(table, index, axis=1, mode="promise_in_bounds")
 
 
-def decode_kernel(own, gate_ids, up_ids, gate_powers, up_powers, gate_b, up_b, gate_a, up_a, out, ids, small, thin, blocks, ready, near, sent):
+def decode_kernel(own, gate_ids, up_ids, gate_powers, up_powers, gate_b, up_b, gate_a, up_a, out, ids, small, thin, ready, near, sent):
     extra, stores = [], []
     for p, (powers, factor, a) in enumerate(((gate_powers, gate_b, gate_a), (up_powers, up_b, up_a))):
         extra.append(pltpu.make_async_copy(powers, small.at[p], near.at[p]))
         extra.append(pltpu.make_async_copy(a, thin.at[p], near.at[2 + p]))
         for h in range(2):
             place = out.at[pl.ds(HELD, 16), pl.ds((2 * p + h) * RANK, RANK)]
-            stores.append(pltpu.make_async_copy(factor.at[pl.ds(h * 16, 16)], place, sent.at[PAIRS + 1 + 2 * p + h]))
+            stores.append(pltpu.make_async_copy(factor.at[pl.ds(h * 16, 16)], place, sent.at[2 * p + h]))
     loads, groups = [], []
     for k in range(GROUPS):
         group = k // 2 * 2 + (own[0] + k % 2) % 2
@@ -73,10 +73,7 @@
     for copy in extra:
         copy.wait()
     rows = jnp.concatenate([thin[0].astype(jnp.float32), thin[1].astype(jnp.float32), jnp.zeros((12, WIDTH), jnp.float32)], axis=0)
-    blocks[pl.ds(HELD, 16), pl.ds(WIDTH, WIDTH)] = rows.astype(jnp.bfloat16)
-    last = (pl.ds(HELD, 16), pl.ds(WIDTH, WIDTH))
-    stores.append(pltpu.make_async_copy(blocks.at[last], out.at[last], sent.at[PAIRS]))
-    stores[-1].start()
+    out[pl.ds(HELD, 16), pl.ds(WIDTH, WIDTH)] = rows.astype(jnp.bfloat16)
     half = lax.broadcasted_iota(jnp.int32, (ROWS, LANES), 1) // BLOCK
     scales = [(jnp.int32(1) << (small[p] + 8)).astype(jnp.float32) * 2.0**-8 for p in range(2)]
     for k in range(GROUPS):
@@ -87,11 +84,7 @@
                 level = pick(ids[p, k, :, pl.ds(chunk * LANES, LANES)].astype(jnp.int16), 0, len(LEVELS))
                 scale = lookup(scales[p], half + (groups[k] * (WIDTH // BLOCK) + chunk * (LANES // BLOCK)))
                 columns = pl.ds(k % 2 * WIDTH + chunk * LANES, LANES)
-                blocks[rows, columns] = level * scale.astype(jnp.bfloat16)
-        if k % 2:
-            rows = pl.ds(k // 2 * 2 * ROWS, 2 * ROWS)
-            stores.append(pltpu.make_async_copy(blocks.at[rows], out.at[rows], sent.at[k // 2]))
-            stores[-1].start()
+                out[rows, columns] = level * scale.astype(jnp.bfloat16)
     for store in stores:
         store.wait()
 
@@ -102,16 +95,15 @@
     return pl.pallas_call(
         decode_kernel,
         in_specs=[pl.BlockSpec(memory_space=pltpu.SMEM)] + [hbm] * 8,
-        out_specs=hbm,
+        out_specs=pl.BlockSpec(memory_space=pltpu.VMEM),
         out_shape=jax.ShapeDtypeStruct(shape, jnp.bfloat16),
         scratch_shapes=[
             pltpu.VMEM((2, GROUPS, ROWS, WIDTH), jnp.int32),
             pltpu.VMEM((2, ROWS, LANES), jnp.int32),
             pltpu.VMEM((2, 2, WIDTH), jnp.bfloat16),
-            pltpu.VMEM(shape, jnp.bfloat16),
             pltpu.SemaphoreType.DMA((2, GROUPS)),
             pltpu.SemaphoreType.DMA((4,)),
-            pltpu.SemaphoreType.DMA((PAIRS + 5,)),
+            pltpu.SemaphoreType.DMA((4,)),
         ],
         compiler_params=pltpu.CompilerParams(vmem_limit_bytes=62 * 2**20),
         cost_estimate=pl.CostEstimate(flops=2**24, bytes_accessed=3 * 2**20, transcendentals=0),

time: 64.6 us -> 64.5 us (level)
  no operation moved by 1% of the time
where the time goes in v7:
time: 64.5 us; the launch traced here: 64.2 us
  blocking collectives  41 us (64%)
  starting transfers between devices  11 us (17%)
  Pallas kernels  9.28 us (14%)
  waiting for transfers between devices  2.35 us (4%)
    all_to_all x1, blocking collectives, exchange_weights(): weights = lax.all_to_all(weights, 'y', 0, 0, tiled=True)  19.7 us
    all_to_all x1, blocking collectives, base_term(): lax.all_to_all(parts.reshape(GROUPS, TOKENS // GROUPS, -1), TENSOR, 0, 0,...  18.9 us
    ppermute x1, starting transfers between devices, per_device(): other = lax.ppermute(blocks, 'c', [(0, 1), (1, 0)])  5.75 us
    ppermute x1, starting transfers between devices, per_device(): near_tokens = lax.ppermute(tokens, ('xl', 'c', 'xh'), pairs)  5.21 us
    pallas_call x1, Pallas kernels, decode(): pl.pallas_call(decode_kernel, in_specs=[pl.BlockSpec(memory_space=pltpu.S...  3.37 us
    pallas_call x1, Pallas kernels, project_near(): pl.pallas_call(project_near_kernel, in_specs=[place, place, pl.BlockSpec(...  3.18 us
    all_gather x1, blocking collectives, per_device(): return finish(core.reshape(1), mine, lax.all_gather(theirs, 'c', axis=0))  2.46 us
    ppermute x1, waiting for transfers between devices, per_device(): other = lax.ppermute(blocks, 'c', [(0, 1), (1, 0)])  2.35 us
  transfers between devices with their start and end apart: 2, of which 1 were waited for; matrix products, arithmetic and copies ran while one was open for 1% of the time, Pallas kernels for 8%

profile of v7, /device:TPU:1, one launch (start us, length us, event | category | flops | bytes accessed | tf_op | source)
XLA Modules:
  0.0 64.2 jit_solution(12139308444922742005)
XLA Ops:
  0.0 5.2 %collective-permute-start.1 = (bf16[1344,1024]{1,0:T(8,128)(2,1)}, bf16[1344,1024]{1,0:T(8,128)(2,1)}, u32[]{:S(2)}, u32[]{:S(2)}) collective-permute-start(bf16[1344,1024]{1,0:T(8,128)(2,1)} %param.13), channel_id=1, source_target_pairs={{8,265},{9,264},{264,9},{265,8},{10,267},{11,266},{266,11},{267,10... | collective-permute-start | bytes 8257544 | tf_op jit(solution)/shard_map/ppermute | solution.py:349
  5.2 3.4 %decode.1 = bf16[272,2048]{1,0:T(8,128)(2,1)S(1)} custom-call(s32[1]{0:T(128)} %bitcast.5.own, s32[32,8192]{1,0:T(8,128)} %gate_ids.1, s32[32,8192]{1,0:T(8,128)} %up_ids.1, s32[32,128]{1,0:T(8,128)} %gate_powers.1, s32[32,128]{1,0:T(8,128)} %up_powers.1, bf16[32,128]{1,0:T(8,128)(2,1)} %gate_b.1, bf16[32,128]{1,0:T(8,128)(2,1)} %up_b.1, ...), custom_call_target="tpu_custom_call" | custom-call | flops 16777216 | bytes 3145728 | tf_op jit(solution)/shard_map/decode/pallas_call | solution.py:95
  8.6 5.7 %collective-permute-start = (bf16[272,2048]{1,0:T(8,128)(2,1)S(1)}, bf16[272,2048]{1,0:T(8,128)(2,1)S(1)}, u32[]{:S(2)}, u32[]{:S(2)}) collective-permute-start(bf16[272,2048]{1,0:T(8,128)(2,1)S(1)} %decode.1), channel_id=1, source_target_pairs={{0,8},{8,0},{1,9},{9,1},{2,10},{10,2},{3,11},{11,3},{4,12},{12,4},... | collective-permute-start | bytes 3342344 | tf_op jit(solution)/shard_map/ppermute | solution.py:352
  14.4 2.4 %collective-permute-done = bf16[272,2048]{1,0:T(8,128)(2,1)S(1)} collective-permute-done((bf16[272,2048]{1,0:T(8,128)(2,1)S(1)}, bf16[272,2048]{1,0:T(8,128)(2,1)S(1)}, u32[]{:S(2)}, u32[]{:S(2)}) %collective-permute-start) | collective-permute-done | bytes 1114144 | tf_op jit(solution)/shard_map/ppermute | solution.py:352
  16.7 21.9 %conditional.2 = (f32[1344,512]{1,0:T(8,128)S(1)}, bf16[512,1024]{1,0:T(8,128)(2,1)S(1)}, bf16[8,144,128]{2,1,0:T(8,128)(2,1)S(1)}) conditional(s32[]{:T(128)} %convert_element_type.4, (bf16[272,2048]{1,0:T(8,128)(2,1)S(1)}, bf16[272,2048]{1,0:T(8,128)(2,1)S(1)}, bf16[1344,1024]{1,0:T(8,128)(2,1)}) %tuple.23, (bf16[1344,1024]{1,0:T(8,128)(2,1)}, ...), branch_computations={%region_0.0_spmd, %region_1.0_spmd} | conditional | flops 1413480448 | bytes 32276534 | solution.py:353
  16.7 0.1 slice.4
  16.8 0.1 slice.5
  16.9 0.2 pad_maximum_fusion
  17.1 0.0 copy-start
  17.2 19.7 %all_to_all.16.weights = bf16[4,128,2048]{2,1,0:T(8,128)(2,1)S(1)} all-to-all(bf16[4,128,2048]{2,1,0:T(8,128)(2,1)S(1)} %pad_maximum_fusion), channel_id=1, replica_groups=mesh['xl'=2,'z'=16,'c'=2,'y'=4,'xh'=2] {'y'}, dimensions={0} | all-to-all | bytes 4194304 | tf_op jit(solution)/shard_map/cond/branch_0_fun/all_to_all | solution.py:325
  36.8 0.0 copy-done
  36.8 1.7 %project_own.1 = (f32[1344,512]{1,0:T(8,128)S(1)}, bf16[512,1024]{1,0:T(8,128)(2,1)S(1)}) custom-call(bf16[4,128,2048]{2,1,0:T(8,128)(2,1)S(1)} %all_to_all.16.weights, bf16[1344,1024]{1,0:T(8,128)(2,1)S(1)} %copy-done), custom_call_target="tpu_custom_call" | custom-call | flops 1409286144 | bytes 8388608 | tf_op jit(solution)/shard_map/cond/branch_0_fun/project_own/pallas_call | solution.py:128
  38.6 0.0 collective-permute-done.1
  38.6 22.3 %conditional.3 = ((f32[168,512]{1,0:T(8,128)S(1)}, bf16[168,512]{1,0:T(8,128)(2,1)S(1)})) conditional(s32[]{:T(128)} %convert_element_type.4, (f32[1344,512]{1,0:T(8,128)S(1)}, bf16[512,1024]{1,0:T(8,128)(2,1)S(1)}, bf16[1344,1024]{1,0:T(8,128)(2,1)}) %tuple.25, bf16[8,144,128]{2,1,0:T(8,128)(2,1)S(1)} %get-tuple-element.46), branch_computations={%region_2.0_spmd, %region_3.0_spmd} | conditional | flops 1411383296 | bytes 14286856 | solution.py:354
  38.6 3.2 %project_near.1 = bf16[1344,512]{1,0:T(8,128)(2,1)S(1)} custom-call(f32[1344,512]{1,0:T(8,128)S(1)} %get-tuple-element.36.total, bf16[512,1024]{1,0:T(8,128)(2,1)S(1)} %get-tuple-element.37.weights, bf16[1344,1024]{1,0:T(8,128)(2,1)} %get-tuple-element.38.tokens), custom_call_target="tpu_custom_call" | custom-call | flops 1409286144 | bytes 8388608 | tf_op jit(solution)/shard_map/cond/branch_0_fun/project_near/pallas_call | solution.py:159
  41.8 18.9 %all_to_all.18.parts = bf16[8,168,512]{2,1,0:T(8,128)(2,1)S(1)} all-to-all(bf16[8,168,512]{2,1,0:T(8,128)(2,1)S(1)} %bitcast.7), channel_id=1, replica_groups=mesh['xl'=2,'z'=16,'c'=2,'y'=4,'xh'=2] {'y','xh'}, dimensions={0} | all-to-all | bytes 2752512 | tf_op jit(solution)/shard_map/cond/branch_0_fun/all_to_all | solution.py:336
  60.7 0.2 add_up.1
  60.9 2.5 %all-gather = bf16[336,512]{1,0:T(8,128)(2,1)S(1)} all-gather(bf16[168,512]{1,0:T(8,128)(2,1)S(1)} %get-tuple-element.48), channel_id=2, replica_groups=mesh['xl'=2,'z'=16,'c'=2,'y'=4,'xh'=2] {'c'}, dimensions={0}, use_global_device_ids=true | all-gather | bytes 516096 | tf_op jit(solution)/shard_map/all_gather | solution.py:355
  63.3 0.9 %finish.1 = bf16[168,256]{1,0:T(8,128)(2,1)} custom-call(s32[1]{0:T(128)} %bitcast.4.core, f32[168,512]{1,0:T(8,128)S(1)} %get-tuple-element.47.mine, bf16[2,168,512]{2,1,0:T(8,128)(2,1)S(1)} %bitcast.8), custom_call_target="tpu_custom_call" | custom-call | flops 1048576 | bytes 1572864 | tf_op jit(solution)/shard_map/finish/pallas_call | solution.py:312
  (1 shorter events, 0.0 us)
Async XLA Ops:
  0.0 38.6 %collective-permute-start.1 = (bf16[1344,1024]{1,0:T(8,128)(2,1)}, bf16[1344,1024]{1,0:T(8,128)(2,1)}, u32[]{:S(2)}, u32[]{:S(2)}) collective-permute-start(bf16[1344,1024]{1,0:T(8,128)(2,1)} %param.13), channel_id=1, source_target_pairs={{8,265},{9,264},{264,9},{265,8},{10,267},{11,266},{266,11},{267,10... | collective-permute-start | bytes 8257544 | tf_op jit(solution)/shard_map/ppermute | solution.py:349
  8.6 8.1 %collective-permute-start = (bf16[272,2048]{1,0:T(8,128)(2,1)S(1)}, bf16[272,2048]{1,0:T(8,128)(2,1)S(1)}, u32[]{:S(2)}, u32[]{:S(2)}) collective-permute-start(bf16[272,2048]{1,0:T(8,128)(2,1)S(1)} %decode.1), channel_id=1, source_target_pairs={{0,8},{8,0},{1,9},{9,1},{2,10},{10,2},{3,11},{11,3},{4,12},{12,4},... | collective-permute-start | bytes 3342344 | tf_op jit(solution)/shard_map/ppermute | solution.py:352
  17.1 19.7 %copy-start = (bf16[1344,1024]{1,0:T(8,128)(2,1)S(1)}, bf16[1344,1024]{1,0:T(8,128)(2,1)}, u32[]{:S(2)}) copy-start(bf16[1344,1024]{1,0:T(8,128)(2,1)} %get-tuple-element.27.tokens) | copy-start | bytes 8257540 | tf_op jit(solution)/shard_map/cond

commit v8 on v7

--- a/solution.py
+++ b/solution.py
@@ -170,13 +170,16 @@
 
 def add_up_kernel(parts, mine, theirs):
     part = PAIRS * ROWS
+    totals = []
     for x in range(2):
         total = parts[x].astype(jnp.float32)
         for y in range(1, PAIRS):
             total = total + parts[2 * y + x].astype(jnp.float32)
-        for q in range(4):
-            to = theirs if q < 2 else mine
-            to[:, pl.ds((q % 2 * 2 + x) * part, part)] = total[:, q * part : (q + 1) * part].astype(to.dtype)
+        totals.append(total)
+    for q in range(4):
+        to = theirs if q < 2 else mine
+        pieces = [totals[x][:, q * part + y * ROWS : q * part + (y + 1) * ROWS] for y in range(PAIRS) for x in range(2)]
+        to[:, pl.ds(q % 2 * 2 * part, 2 * part)] = jnp.concatenate(pieces, axis=1).astype(to.dtype)
 
 
 def add_up(parts):
@@ -249,7 +252,7 @@
     owner = slot // 2 % 2 * 32 + slot // 4 * 2 + slot % 2
     for q in range(4):
         hit = (place % 4 // 2 == q % 2) & (owner * 2 + place % 2 == rank)
-        factor = jnp.concatenate([side[k, pl.ds(q * ROWS, ROWS), :] for k in (0, 2, 4, 6, 1, 3, 5, 7)], axis=0)
+        factor = jnp.concatenate([side[k, pl.ds(q * ROWS, ROWS), :] for k in range(GROUPS)], axis=0)
         out[q] = jnp.dot(
             factor, hit.astype(jnp.float32).astype(jnp.bfloat16), preferred_element_type=jnp.float32
         ).astype(jnp.bfloat16)
@@ -298,13 +301,7 @@
     other = both.at[1 - core[0]]
     gate = mine[:, :half] + other[:, :half].astype(jnp.float32)
     up = mine[:, half:] + other[:, half:].astype(jnp.float32)
-    result = (gate / (1.0 + jnp.exp(-gate)) * up).astype(jnp.bfloat16)
-    place = lax.broadcasted_iota(jnp.int32, (half, half), 0)
-    column = lax.broadcasted_iota(jnp.int32, (half, half), 1)
-    group = column // ROWS
-    wanted = (group % 2 * PAIRS + group // 2) * ROWS + column % ROWS
-    move = (place == wanted).astype(jnp.float32).astype(jnp.bfloat16)
-    out[...] = jnp.dot(result, move, preferred_element_type=jnp.float32).astype(jnp.bfloat16)
+    out[...] = (gate / (1.0 + jnp.exp(-gate)) * up).astype(jnp.bfloat16)
 
 
 def finish(core, mine, both):

time: 64.5 us -> 64.4 us (level)
  no operation moved by 1% of the time
where the time goes in v8:
time: 64.4 us; the launch traced here: 64.1 us
  blocking collectives  40.7 us (63%)
  starting transfers between devices  11 us (17%)
  Pallas kernels  9.45 us (15%)
  waiting for transfers between devices  2.35 us (4%)
    all_to_all x1, blocking collectives, exchange_weights(): weights = lax.all_to_all(weights, 'y', 0, 0, tiled=True)  19.7 us
    all_to_all x1, blocking collectives, base_term(): lax.all_to_all(parts.reshape(GROUPS, TOKENS // GROUPS, -1), TENSOR, 0, 0,...  18.9 us
    ppermute x1, starting transfers between devices, per_device(): other = lax.ppermute(blocks, 'c', [(0, 1), (1, 0)])  5.75 us
    ppermute x1, starting transfers between devices, per_device(): near_tokens = lax.ppermute(tokens, ('xl', 'c', 'xh'), pairs)  5.21 us
    pallas_call x1, Pallas kernels, decode(): pl.pallas_call(decode_kernel, in_specs=[pl.BlockSpec(memory_space=pltpu.S...  3.37 us
    pallas_call x1, Pallas kernels, project_near(): pl.pallas_call(project_near_kernel, in_specs=[place, place, pl.BlockSpec(...  3.18 us
    ppermute x1, waiting for transfers between devices, per_device(): other = lax.ppermute(blocks, 'c', [(0, 1), (1, 0)])  2.35 us
    all_gather x1, blocking collectives, per_device(): return finish(core.reshape(1), mine, lax.all_gather(theirs, 'c', axis=0))  2.14 us
  transfers between devices with their start and end apart: 2, of which 1 were waited for; matrix products, arithmetic and copies ran while one was open for 1% of the time, Pallas kernels for 8%

profile of v8, /device:TPU:1, one launch (start us, length us, event | category | flops | bytes accessed | tf_op | source)
XLA Modules:
  0.0 64.1 jit_solution(951454332005434724)
XLA Ops:
  0.0 5.2 %collective-permute-start.1 = (bf16[1344,1024]{1,0:T(8,128)(2,1)}, bf16[1344,1024]{1,0:T(8,128)(2,1)}, u32[]{:S(2)}, u32[]{:S(2)}) collective-permute-start(bf16[1344,1024]{1,0:T(8,128)(2,1)} %param.13), channel_id=1, source_target_pairs={{8,265},{9,264},{264,9},{265,8},{10,267},{11,266},{266,11},{267,10... | collective-permute-start | bytes 8257544 | tf_op jit(solution)/shard_map/ppermute | solution.py:346
  5.2 3.4 %decode.1 = bf16[272,2048]{1,0:T(8,128)(2,1)S(1)} custom-call(s32[1]{0:T(128)} %bitcast.5.own, s32[32,8192]{1,0:T(8,128)} %gate_ids.1, s32[32,8192]{1,0:T(8,128)} %up_ids.1, s32[32,128]{1,0:T(8,128)} %gate_powers.1, s32[32,128]{1,0:T(8,128)} %up_powers.1, bf16[32,128]{1,0:T(8,128)(2,1)} %gate_b.1, bf16[32,128]{1,0:T(8,128)(2,1)} %up_b.1, ...), custom_call_target="tpu_custom_call" | custom-call | flops 16777216 | bytes 3145728 | tf_op jit(solution)/shard_map/decode/pallas_call | solution.py:95
  8.6 5.7 %collective-permute-start = (bf16[272,2048]{1,0:T(8,128)(2,1)S(1)}, bf16[272,2048]{1,0:T(8,128)(2,1)S(1)}, u32[]{:S(2)}, u32[]{:S(2)}) collective-permute-start(bf16[272,2048]{1,0:T(8,128)(2,1)S(1)} %decode.1), channel_id=1, source_target_pairs={{0,8},{8,0},{1,9},{9,1},{2,10},{10,2},{3,11},{11,3},{4,12},{12,4},... | collective-permute-start | bytes 3342344 | tf_op jit(solution)/shard_map/ppermute | solution.py:349
  14.4 2.4 %collective-permute-done = bf16[272,2048]{1,0:T(8,128)(2,1)S(1)} collective-permute-done((bf16[272,2048]{1,0:T(8,128)(2,1)S(1)}, bf16[272,2048]{1,0:T(8,128)(2,1)S(1)}, u32[]{:S(2)}, u32[]{:S(2)}) %collective-permute-start) | collective-permute-done | bytes 1114144 | tf_op jit(solution)/shard_map/ppermute | solution.py:349
  16.7 21.9 %conditional.2 = (f32[1344,512]{1,0:T(8,128)S(1)}, bf16[512,1024]{1,0:T(8,128)(2,1)S(1)}, bf16[8,144,128]{2,1,0:T(8,128)(2,1)S(1)}) conditional(s32[]{:T(128)} %convert_element_type.4, (bf16[272,2048]{1,0:T(8,128)(2,1)S(1)}, bf16[272,2048]{1,0:T(8,128)(2,1)S(1)}, bf16[1344,1024]{1,0:T(8,128)(2,1)}) %tuple.23, (bf16[1344,1024]{1,0:T(8,128)(2,1)}, ...), branch_computations={%region_0.0_spmd, %region_1.0_spmd} | conditional | flops 1413480448 | bytes 32276534 | solution.py:350
  16.7 0.1 slice.4
  16.8 0.1 slice.5
  16.9 0.2 pad_maximum_fusion
  17.1 0.0 copy-start
  17.2 19.7 %all_to_all.16.weights = bf16[4,128,2048]{2,1,0:T(8,128)(2,1)S(1)} all-to-all(bf16[4,128,2048]{2,1,0:T(8,128)(2,1)S(1)} %pad_maximum_fusion), channel_id=1, replica_groups=mesh['xl'=2,'z'=16,'c'=2,'y'=4,'xh'=2] {'y'}, dimensions={0} | all-to-all | bytes 4194304 | tf_op jit(solution)/shard_map/cond/branch_0_fun/all_to_all | solution.py:322
  36.8 0.0 copy-done
  36.8 1.7 %project_own.1 = (f32[1344,512]{1,0:T(8,128)S(1)}, bf16[512,1024]{1,0:T(8,128)(2,1)S(1)}) custom-call(bf16[4,128,2048]{2,1,0:T(8,128)(2,1)S(1)} %all_to_all.16.weights, bf16[1344,1024]{1,0:T(8,128)(2,1)S(1)} %copy-done), custom_call_target="tpu_custom_call" | custom-call | flops 1409286144 | bytes 8388608 | tf_op jit(solution)/shard_map/cond/branch_0_fun/project_own/pallas_call | solution.py:128
  38.6 0.0 collective-permute-done.1
  38.6 22.6 %conditional.3 = ((f32[168,512]{1,0:T(8,128)S(1)}, bf16[168,512]{1,0:T(8,128)(2,1)S(1)})) conditional(s32[]{:T(128)} %convert_element_type.4, (f32[1344,512]{1,0:T(8,128)S(1)}, bf16[512,1024]{1,0:T(8,128)(2,1)S(1)}, bf16[1344,1024]{1,0:T(8,128)(2,1)}) %tuple.25, bf16[8,144,128]{2,1,0:T(8,128)(2,1)S(1)} %get-tuple-element.46), branch_computations={%region_2.0_spmd, %region_3.0_spmd} | conditional | flops 1411383296 | bytes 14286856 | solution.py:351
  38.6 3.2 %project_near.1 = bf16[1344,512]{1,0:T(8,128)(2,1)S(1)} custom-call(f32[1344,512]{1,0:T(8,128)S(1)} %get-tuple-element.36.total, bf16[512,1024]{1,0:T(8,128)(2,1)S(1)} %get-tuple-element.37.weights, bf16[1344,1024]{1,0:T(8,128)(2,1)} %get-tuple-element.38.tokens), custom_call_target="tpu_custom_call" | custom-call | flops 1409286144 | bytes 8388608 | tf_op jit(solution)/shard_map/cond/branch_0_fun/project_near/pallas_call | solution.py:159
  41.8 18.9 %all_to_all.18.parts = bf16[8,168,512]{2,1,0:T(8,128)(2,1)S(1)} all-to-all(bf16[8,168,512]{2,1,0:T(8,128)(2,1)S(1)} %bitcast.7), channel_id=1, replica_groups=mesh['xl'=2,'z'=16,'c'=2,'y'=4,'xh'=2] {'y','xh'}, dimensions={0} | all-to-all | bytes 2752512 | tf_op jit(solution)/shard_map/cond/branch_0_fun/all_to_all | solution.py:333
  60.7 0.5 add_up.1
  61.2 2.1 %all-gather = bf16[336,512]{1,0:T(8,128)(2,1)S(1)} all-gather(bf16[168,512]{1,0:T(8,128)(2,1)S(1)} %get-tuple-element.48), channel_id=2, replica_groups=mesh['xl'=2,'z'=16,'c'=2,'y'=4,'xh'=2] {'c'}, dimensions={0}, use_global_device_ids=true | all-gather | bytes 516096 | tf_op jit(solution)/shard_map/all_gather | solution.py:352
  63.3 0.7 %finish.1 = bf16[168,256]{1,0:T(8,128)(2,1)} custom-call(s32[1]{0:T(128)} %bitcast.4.core, f32[168,512]{1,0:T(8,128)S(1)} %get-tuple-element.47.mine, bf16[2,168,512]{2,1,0:T(8,128)(2,1)S(1)} %bitcast.8), custom_call_target="tpu_custom_call" | custom-call | flops 1048576 | bytes 1572864 | tf_op jit(solution)/shard_map/finish/pallas_call | solution.py:309
  (1 shorter events, 0.0 us)
Async XLA Ops:
  0.0 38.6 %collective-permute-start.1 = (bf16[1344,1024]{1,0:T(8,128)(2,1)}, bf16[1344,1024]{1,0:T(8,128)(2,1)}, u32[]{:S(2)}, u32[]{:S(2)}) collective-permute-start(bf16[1344,1024]{1,0:T(8,128)(2,1)} %param.13), channel_id=1, source_target_pairs={{8,265},{9,264},{264,9},{265,8},{10,267},{11,266},{266,11},{267,10... | collective-permute-start | bytes 8257544 | tf_op jit(solution)/shard_map/ppermute | solution.py:346
  8.6 8.1 %collective-permute-start = (bf16[272,2048]{1,0:T(8,128)(2,1)S(1)}, bf16[272,2048]{1,0:T(8,128)(2,1)S(1)}, u32[]{:S(2)}, u32[]{:S(2)}) collective-permute-start(bf16[272,2048]{1,0:T(8,128)(2,1)S(1)} %decode.1), channel_id=1, source_target_pairs={{0,8},{8,0},{1,9},{9,1},{2,10},{10,2},{3,11},{11,3},{4,12},{12,4},... | collective-permute-start | bytes 3342344 | tf_op jit(solution)/shard_map/ppermute | solution.py:349
  17.1 19.7 %copy-start = (bf16[1344,1024]{1,0:T(8,128)(2,1)S(1)}, bf16[1344,1024]{1,0:T(8,128)(2,1)}, u32[]{:S(2)}) copy-start(bf16[1344,1024]{1,0:T(8,128)(2,1)} %get-tuple-element.27.tokens) | copy-start | bytes 8257540 | tf_op jit(solution)/shard_map/cond

commit v9 on v8

--- a/solution.py
+++ b/solution.py
@@ -114,7 +114,7 @@
 DIMS = (((1,), (1,)), ((), ()))
 
 
-def project_own_kernel(weights, tokens, out, rest, merged):
+def project_own_kernel(weights, tokens, out, rest, room, merged):
     part = PAIRS * ROWS
     for q in range(4):
         merged[pl.ds(q * part, part), :] = weights[:, pl.ds(q * ROWS, ROWS), pl.ds(0, WIDTH)].reshape(part, WIDTH)
@@ -128,10 +128,11 @@
     return pl.pallas_call(
         project_own_kernel,
         in_specs=[place, place],
-        out_specs=[place, place],
+        out_specs=[place, place, pl.BlockSpec(memory_space=pl.ANY)],
         out_shape=[
             jax.ShapeDtypeStruct((TOKENS, columns), jnp.float32),
             jax.ShapeDtypeStruct((columns, WIDTH), jnp.bfloat16),
+            jax.ShapeDtypeStruct((GROUPS, SIDE, LANES), jnp.bfloat16),
         ],
         scratch_shapes=[pltpu.VMEM((columns, WIDTH), jnp.bfloat16)],
         compiler_params=pltpu.CompilerParams(vmem_limit_bytes=32 * 2**20),
@@ -320,7 +321,7 @@
 def exchange_weights(blocks, other, tokens):
     weights = jnp.concatenate([part[:HELD].reshape(PAIRS, 2 * ROWS, 2 * WIDTH) for part in (other, blocks)], axis=1)
     weights = lax.all_to_all(weights, "y", 0, 0, tiled=True)
-    return *project_own(weights, tokens), jnp.zeros((GROUPS, SIDE, LANES), jnp.bfloat16)
+    return tuple(project_own(weights, tokens))
 
 
 def exchange_shrunk(blocks, other, tokens):

time: 64.4 us -> 65.9 us (1.023)
  Pallas kernels: 9.45 us -> 13.4 us
  blocking collectives: 40.7 us -> 38.4 us
    all_to_all x1, blocking collectives: 18.9 us -> 16.7 us  [base_term(): lax.all_to_all(parts.reshape(GROUPS, TOKENS // GROUPS, -1), TENSOR, 0, 0,...]
    pallas_call x1, Pallas kernels: 3.18 us -> 5.23 us  [project_near(): pl.pallas_call(project_near_kernel, in_specs=[place, place, pl.BlockSpec(...]
    pallas_call x1, Pallas kernels: 1.69 us -> 3.54 us  [project_own(): pl.pallas_call(project_own_kernel, in_specs=[place, place], out_specs=[pl...]
  transfers between devices with their start and end apart: 2 -> 2, of which waited for: 1 -> 1; matrix products, arithmetic and copies ran while one was open for 1% -> 1% of each run, Pallas kernels for 8% -> 11%
where the time goes in v9:
time: 65.9 us; the launch traced here: 65.6 us
  blocking collectives  38.4 us (58%)
  Pallas kernels  13.4 us (20%)
  starting transfers between devices  11 us (17%)
  waiting for transfers between devices  2.35 us (4%)
    all_to_all x1, blocking collectives, exchange_weights(): weights = lax.all_to_all(weights, 'y', 0, 0, tiled=True)  19.7 us
    all_to_all x1, blocking collectives, base_term(): lax.all_to_all(parts.reshape(GROUPS, TOKENS // GROUPS, -1), TENSOR, 0, 0,...  16.7 us
    ppermute x1, starting transfers between devices, per_device(): other = lax.ppermute(blocks, 'c', [(0, 1), (1, 0)])  5.75 us
    pallas_call x1, Pallas kernels, project_near(): pl.pallas_call(project_near_kernel, in_specs=[place, place, pl.BlockSpec(...  5.23 us
    ppermute x1, starting transfers between devices, per_device(): near_tokens = lax.ppermute(tokens, ('xl', 'c', 'xh'), pairs)  5.21 us
    pallas_call x1, Pallas kernels, project_own(): pl.pallas_call(project_own_kernel, in_specs=[place, place], out_specs=[pl...  3.54 us
    pallas_call x1, Pallas kernels, decode(): pl.pallas_call(decode_kernel, in_specs=[pl.BlockSpec(memory_space=pltpu.S...  3.37 us
    ppermute x1, waiting for transfers between devices, per_device(): other = lax.ppermute(blocks, 'c', [(0, 1), (1, 0)])  2.35 us
  transfers between devices with their start and end apart: 2, of which 1 were waited for; matrix products, arithmetic and copies ran while one was open for 1% of the time, Pallas kernels for 11%

profile of v9, /device:TPU:1, one launch (start us, length us, event | category | flops | bytes accessed | tf_op | source)
XLA Modules:
  0.0 65.6 jit_solution(12941771369222391669)
XLA Ops:
  0.0 5.2 %collective-permute-start.1 = (bf16[1344,1024]{1,0:T(8,128)(2,1)}, bf16[1344,1024]{1,0:T(8,128)(2,1)}, u32[]{:S(2)}, u32[]{:S(2)}) collective-permute-start(bf16[1344,1024]{1,0:T(8,128)(2,1)} %param.13), channel_id=1, source_target_pairs={{8,265},{9,264},{264,9},{265,8},{10,267},{11,266},{266,11},{267,10... | collective-permute-start | bytes 8257544 | tf_op jit(solution)/shard_map/ppermute | solution.py:347
  5.2 3.4 %decode.1 = bf16[272,2048]{1,0:T(8,128)(2,1)S(1)} custom-call(s32[1]{0:T(128)} %bitcast.5.own, s32[32,8192]{1,0:T(8,128)} %gate_ids.1, s32[32,8192]{1,0:T(8,128)} %up_ids.1, s32[32,128]{1,0:T(8,128)} %gate_powers.1, s32[32,128]{1,0:T(8,128)} %up_powers.1, bf16[32,128]{1,0:T(8,128)(2,1)} %gate_b.1, bf16[32,128]{1,0:T(8,128)(2,1)} %up_b.1, ...), custom_call_target="tpu_custom_call" | custom-call | flops 16777216 | bytes 3145728 | tf_op jit(solution)/shard_map/decode/pallas_call | solution.py:95
  8.6 5.7 %collective-permute-start = (bf16[272,2048]{1,0:T(8,128)(2,1)S(1)}, bf16[272,2048]{1,0:T(8,128)(2,1)S(1)}, u32[]{:S(2)}, u32[]{:S(2)}) collective-permute-start(bf16[272,2048]{1,0:T(8,128)(2,1)S(1)} %decode.1), channel_id=1, source_target_pairs={{0,8},{8,0},{1,9},{9,1},{2,10},{10,2},{3,11},{11,3},{4,12},{12,4},... | collective-permute-start | bytes 3342344 | tf_op jit(solution)/shard_map/ppermute | solution.py:350
  14.4 2.4 %collective-permute-done = bf16[272,2048]{1,0:T(8,128)(2,1)S(1)} collective-permute-done((bf16[272,2048]{1,0:T(8,128)(2,1)S(1)}, bf16[272,2048]{1,0:T(8,128)(2,1)S(1)}, u32[]{:S(2)}, u32[]{:S(2)}) %collective-permute-start) | collective-permute-done | bytes 1114144 | tf_op jit(solution)/shard_map/ppermute | solution.py:350
  16.7 23.7 %conditional.2 = ((f32[1344,512]{1,0:T(8,128)}, bf16[512,1024]{1,0:T(8,128)(2,1)}, bf16[8,144,128]{2,1,0:T(8,128)(2,1)S(1)})) conditional(s32[]{:T(128)} %convert_element_type.4, (bf16[272,2048]{1,0:T(8,128)(2,1)S(1)}, bf16[272,2048]{1,0:T(8,128)(2,1)S(1)}, bf16[1344,1024]{1,0:T(8,128)(2,1)}) %tuple.22, (bf16[1344,1024]{1,0:T(8,128)(2,1)}, ...), branch_computations={%region_0.0_spmd, %region_1.0_spmd} | conditional | flops 1413480448 | bytes 31981604 | solution.py:351
  16.7 0.1 slice.4
  16.8 0.1 slice.5
  16.9 0.2 pad_maximum_fusion
  17.1 0.0 copy-start
  17.2 19.7 %all_to_all.16.weights = bf16[4,128,2048]{2,1,0:T(8,128)(2,1)S(1)} all-to-all(bf16[4,128,2048]{2,1,0:T(8,128)(2,1)S(1)} %pad_maximum_fusion), channel_id=1, replica_groups=mesh['xl'=2,'z'=16,'c'=2,'y'=4,'xh'=2] {'y'}, dimensions={0} | all-to-all | bytes 4194304 | tf_op jit(solution)/shard_map/cond/branch_0_fun/all_to_all | solution.py:323
  36.8 0.0 copy-done
  36.8 3.5 %project_own.1 = (f32[1344,512]{1,0:T(8,128)}, bf16[512,1024]{1,0:T(8,128)(2,1)}, bf16[8,144,128]{2,1,0:T(8,128)(2,1)S(1)}) custom-call(bf16[4,128,2048]{2,1,0:T(8,128)(2,1)S(1)} %all_to_all.16.weights, bf16[1344,1024]{1,0:T(8,128)(2,1)S(1)} %copy-done), custom_call_target="tpu_custom_call" | custom-call | flops 1409286144 | bytes 8388608 | tf_op jit(solution)/shard_map/cond/branch_0_fun/project_own/pallas_call | solution.py:128
  40.4 0.0 collective-permute-done.1
  40.4 22.5 %conditional.3 = ((f32[168,512]{1,0:T(8,128)S(1)}, bf16[168,512]{1,0:T(8,128)(2,1)S(1)})) conditional(s32[]{:T(128)} %convert_element_type.4, (f32[1344,512]{1,0:T(8,128)}, bf16[512,1024]{1,0:T(8,128)(2,1)}, bf16[1344,1024]{1,0:T(8,128)(2,1)}) %tuple.24, bf16[8,144,128]{2,1,0:T(8,128)(2,1)S(1)} %get-tuple-element.47), branch_computations={%region_2.0_spmd, %region_3.0_spmd} | conditional | flops 1411383296 | bytes 14286856 | solution.py:352
  40.4 5.2 %project_near.1 = bf16[1344,512]{1,0:T(8,128)(2,1)S(1)} custom-call(f32[1344,512]{1,0:T(8,128)} %get-tuple-element.37.total, bf16[512,1024]{1,0:T(8,128)(2,1)} %get-tuple-element.38.weights, bf16[1344,1024]{1,0:T(8,128)(2,1)} %get-tuple-element.39.tokens), custom_call_target="tpu_custom_call" | custom-call | flops 1409286144 | bytes 8388608 | tf_op jit(solution)/shard_map/cond/branch_0_fun/project_near/pallas_call | solution.py:160
  45.6 16.7 %all_to_all.18.parts = bf16[8,168,512]{2,1,0:T(8,128)(2,1)S(1)} all-to-all(bf16[8,168,512]{2,1,0:T(8,128)(2,1)S(1)} %bitcast.7), channel_id=1, replica_groups=mesh['xl'=2,'z'=16,'c'=2,'y'=4,'xh'=2] {'y','xh'}, dimensions={0} | all-to-all | bytes 2752512 | tf_op jit(solution)/shard_map/cond/branch_0_fun/all_to_all | solution.py:334
  62.3 0.5 add_up.1
  62.8 2.1 %all-gather = bf16[336,512]{1,0:T(8,128)(2,1)S(1)} all-gather(bf16[168,512]{1,0:T(8,128)(2,1)S(1)} %get-tuple-element.49), channel_id=2, replica_groups=mesh['xl'=2,'z'=16,'c'=2,'y'=4,'xh'=2] {'c'}, dimensions={0}, use_global_device_ids=true | all-gather | bytes 516096 | tf_op jit(solution)/shard_map/all_gather | solution.py:353
  64.9 0.7 %finish.1 = bf16[168,256]{1,0:T(8,128)(2,1)} custom-call(s32[1]{0:T(128)} %bitcast.4.core, f32[168,512]{1,0:T(8,128)S(1)} %get-tuple-element.48.mine, bf16[2,168,512]{2,1,0:T(8,128)(2,1)S(1)} %bitcast.8), custom_call_target="tpu_custom_call" | custom-call | flops 1048576 | bytes 1572864 | tf_op jit(solution)/shard_map/finish/pallas_call | solution.py:310
Async XLA Ops:
  0.0 40.4 %collective-permute-start.1 = (bf16[1344,1024]{1,0:T(8,128)(2,1)}, bf16[1344,1024]{1,0:T(8,128)(2,1)}, u32[]{:S(2)}, u32[]{:S(2)}) collective-permute-start(bf16[1344,1024]{1,0:T(8,128)(2,1)} %param.13), channel_id=1, source_target_pairs={{8,265},{9,264},{264,9},{265,8},{10,267},{11,266},{266,11},{267,10... | collective-permute-start | bytes 8257544 | tf_op jit(solution)/shard_map/ppermute | solution.py:347
  8.6 8.1 %collective-permute-start = (bf16[272,2048]{1,0:T(8,128)(2,1)S(1)}, bf16[272,2048]{1,0:T(8,128)(2,1)S(1)}, u32[]{:S(2)}, u32[]{:S(2)}) collective-permute-start(bf16[272,2048]{1,0:T(8,128)(2,1)S(1)} %decode.1), channel_id=1, source_target_pairs={{0,8},{8,0},{1,9},{9,1},{2,10},{10,2},{3,11},{11,3},{4,12},{12,4},... | collective-permute-start | bytes 3342344 | tf_op jit(solution)/shard_map/ppermute | solution.py:350
  17.1 19.7 %copy-start = (bf16[1344,1024]{1,0:T(8,128)(2,1)S(1)}, bf16[1344,1024]{1,0:T(8,128)(2,1)}, u32[]{:S(2)}) copy-start(bf16[1344,1024]{1,0:T(8,128)(2,1)} %get-tuple-element.30.tokens) | copy-start | bytes 8257540 | tf_op jit(solution)/shard_map/cond
